TPU v7x, 32 devices: a whole 2x2x4 slice. The times are simulated.
32 devices in a mesh: gx: 2 (over core), gy: 4 (over y, x), gz: 4 (over z).
Axes of the slice: x: 2, y: 2, z: 4, core: 2. Of those that a mesh axis runs over, the one named last changes fastest.
Arguments:
- velocity: float32 [3, 16, 128, 512], P(None, 'gx', 'gy', 'gz'), may hold values from -6 to 6
- nu_tilde: float32 [16, 128, 512], P('gx', 'gy', 'gz'), may hold values from 0.05 to 2
- fluid_cells: int32 [16, 128, 512], P('gx', 'gy', 'gz'), may hold values 0 or 1
- surface: float32 [2, 4, 3, 512], P('gx', 'gz', None, 'gy'), may hold values from -64 to 64
- pitch_angle: float32 [1], replicated, may hold values from -0.15 to 0.15
- near_tiles: int32 [2, 4, 4, 8], P('gx', 'gy', 'gz'), may hold values from -1 to 31, as said below
- send_rows: int32 [2, 4, 4, 8, 128], P('gx', 'gy', 'gz'), may hold values from -1 to 32767, as said below
- ghost_cell: int32 [2, 4, 4, 2048], P('gx', 'gy', 'gz'), may hold values from 0 to 32767, as said below
- ghost_src: int32 [2, 4, 4, 8, 2048], P('gx', 'gy', 'gz'), may hold values from 0 to 1023, as said below
- ghost_weight: float32 [2, 4, 4, 8, 2048], P('gx', 'gy', 'gz'), may hold values from 0 to 1, as said below
Outputs:
- new_velocity: float32 [3, 16, 128, 512], P(None, 'gx', 'gy', 'gz')
- new_nu_tilde: float32 [16, 128, 512], P('gx', 'gy', 'gz')
- wall_distance: float32 [16, 128, 512], P('gx', 'gy', 'gz')
Inputs may be any that keep to these rules, and one draw needn't show every extreme that they name: `send_rows`: in each list of 128 slots from one device to one peer of gx+gz, live entries (local cell numbers of the sender) come first and the rest are -1. In every spanwise index some peer receives 128 live rows from every device. `ghost_src`: p * 128 + s names slot s of the rows that peer p sends to this device; it always names a live slot. `ghost_cell`: the 2048 entries of one device are distinct. `near_tiles`: distinct tiles first, the rest -1; some device lists 8 tiles. `ghost_weight`: the weights of one image point are non-negative and sum to one.
All inputs are finite; a program needn't handle non-finite values. No bound on the sum of `fluid_cells` on one device may be relied on, other than what follows from the above.
Results may differ from a plain program's by a relative error of at most 0.0003.
Values sent between devices are 32-bit elements; how exact they have to be, the bound alone decides.
A program may use at most 128 MiB of HBM per device.

v0:
```python
import jax
import jax.numpy as jnp
from jax import lax
from jax.sharding import PartitionSpec as P

TY = 8


viscosity = 0.2
prod_coef = 0.1355
grad_coef = 0.622
sigma_inv = 1.5
karman = 0.41
visc_coef = 7.1
wall_coef = prod_coef / (karman * karman) + (1.0 + grad_coef) * sigma_inv
des_coef = 0.65
floor_rate = 0.3
dist_eps = 0.25
dist_cap = 8.0
time_step = 0.05


def with_halo(block, sides, width):
    for axis, dim in sides:
        count = lax.axis_size(axis)
        forward = [(i, i + 1) for i in range(count - 1)]
        backward = [(target, source) for source, target in forward]
        low = lax.ppermute(
            lax.slice_in_dim(block, block.shape[dim] - width, None, axis=dim), axis, forward
        )
        high = lax.ppermute(lax.slice_in_dim(block, 0, width, axis=dim), axis, backward)
        block = jnp.concatenate([low, block, high], axis=dim)
    return block


def rotate(points, pitch_angle):
    cosine = jnp.cos(pitch_angle[0])
    sine_value = jnp.sin(pitch_angle[0])
    turned_x = cosine * points[0] + sine_value * points[2]
    turned_z = cosine * points[2] - sine_value * points[0]
    return jnp.stack([turned_x, points[1], turned_z])


def cell_coords(tile_list, y_offset, total_span, cells_x, cells_y, cells_z):
    per_row = cells_y // TY
    slots = tile_list.shape[0]
    safe_tiles = jnp.maximum(tile_list, 0)
    plane_index = (safe_tiles // per_row).astype(jnp.float32)
    band_row = safe_tiles % per_row * TY + y_offset
    row_index = band_row[:, None] + jnp.arange(TY, dtype=jnp.int32)[None, :]
    coord_x = jnp.broadcast_to(
        (plane_index + 0.5 - 0.5 * cells_x)[:, None, None], (slots, TY, cells_z)
    )
    coord_y = jnp.broadcast_to(
        (row_index.astype(jnp.float32) + 0.5 - 0.5 * total_span)[:, :, None], (slots, TY, cells_z)
    )
    depth = jnp.arange(cells_z, dtype=jnp.int32).astype(jnp.float32) + 0.5 - 0.5 * cells_z
    coord_z = jnp.broadcast_to(depth[None, None, :], (slots, TY, cells_z))
    return jnp.stack([coord_x, coord_y, coord_z]).reshape(3, slots, TY * cells_z)


def closest(cell_list, points, nearest_sq):

    def one_slot(slot_pair):
        slot_cells, best_now = slot_pair
        step_x = slot_cells[0][:, None] - points[0][None, :]
        step_y = slot_cells[1][:, None] - points[1][None, :]
        step_z = slot_cells[2][:, None] - points[2][None, :]
        squared = step_x * step_x + step_y * step_y + step_z * step_z
        return jnp.minimum(best_now, jnp.min(squared, axis=1))

    return lax.map(one_slot, (jnp.moveaxis(cell_list, 1, 0), nearest_sq))


def place_tiles(tile_list, values, cells_x, cells_y, cells_z):
    tile_count = cells_x * (cells_y // TY)
    tile_grid = jnp.full((tile_count, TY * cells_z), dist_cap, jnp.float32)
    target = jnp.where(tile_list >= 0, tile_list, tile_count)
    tile_grid = tile_grid.at[target].set(values, mode="drop")
    return tile_grid.reshape(cells_x, cells_y, cells_z)


def neighbour(padded, direction, offset, interior):
    slices = [slice(None)]
    for dimension in range(3):
        begin = 2 + (offset if dimension == direction else 0)
        slices.append(slice(begin, begin + interior[dimension]))
    return padded[tuple(slices)]


def advance(padded, wall_dist, fluid_cells):
    interior = (padded.shape[1] - 4, padded.shape[2] - 4, padded.shape[3] - 4)
    center = neighbour(padded, 0, 0, interior)
    gradient = []
    laplace = jnp.zeros_like(center)
    for direction in range(3):
        plus_one = neighbour(padded, direction, 1, interior)
        minus_one = neighbour(padded, direction, -1, interior)
        plus_two = neighbour(padded, direction, 2, interior)
        minus_two = neighbour(padded, direction, -2, interior)
        gradient.append((minus_two - plus_two + 8.0 * (plus_one - minus_one)) / 12.0)
        laplace = laplace + (plus_one + minus_one - 2.0 * center)
    moving = center[:3]
    working = center[3]
    curl_x = gradient[1][2] - gradient[2][1]
    curl_y = gradient[2][0] - gradient[0][2]
    curl_z = gradient[0][1] - gradient[1][0]
    vort_rate = jnp.maximum(
        jnp.sqrt(curl_x * curl_x + curl_y * curl_y + curl_z * curl_z), floor_rate
    )
    positive = jnp.maximum(working, 0.0)
    chi_ratio = positive / viscosity
    chi_cubed = chi_ratio * chi_ratio * chi_ratio
    eddy_visc = positive * chi_cubed / (chi_cubed + visc_coef**3)
    diffusion = viscosity + eddy_visc
    shield_arg = diffusion / (vort_rate * karman * karman * wall_dist * wall_dist)
    shield = 1.0 - jnp.tanh((8.0 * shield_arg) ** 3)
    length = wall_dist - shield * jnp.maximum(wall_dist - des_coef, 0.0)
    convect = moving[0] * gradient[0] + moving[1] * gradient[1] + moving[2] * gradient[2]
    grad_sq = (
        gradient[0][3] * gradient[0][3]
        + gradient[1][3] * gradient[1][3]
        + gradient[2][3] * gradient[2][3]
    )
    nu_rhs = (
        -convect[3]
        + sigma_inv * ((viscosity + positive) * laplace[3] + grad_coef * grad_sq)
        + prod_coef * vort_rate * working
        - wall_coef * working * jnp.abs(working) / (length * length)
    )
    vel_rhs = -convect[:3] + diffusion[None] * laplace[:3]
    fluid_mask = fluid_cells.astype(jnp.float32)
    new_velocity = moving + time_step * fluid_mask[None] * vel_rhs
    new_nu = working + time_step * fluid_mask * nu_rhs
    return (new_velocity, new_nu)


def on_device(
    velocity,
    nu_tilde,
    fluid_cells,
    surface,
    pitch_angle,
    near_tiles,
    send_rows,
    ghost_cell,
    ghost_src,
    ghost_weight,
):
    cells_x = velocity.shape[1]
    cells_y = velocity.shape[2]
    cells_z = velocity.shape[3]
    fields = jnp.concatenate([velocity, nu_tilde[None]], axis=0)
    flat_state = fields.reshape(4, cells_x * cells_y * cells_z)
    row_list = send_rows[0, 0, 0]
    live_rows = row_list >= 0
    outgoing = jnp.where(live_rows[None], flat_state[:, jnp.where(live_rows, row_list, 0)], 0.0)
    incoming = lax.all_to_all(outgoing, ("gx", "gz"), split_axis=1, concat_axis=1, tiled=True)
    buffer = incoming.reshape(4, incoming.shape[1] * incoming.shape[2])
    values = buffer[:, ghost_src[0, 0, 0]]
    ghost_value = -jnp.sum(ghost_weight[0, 0, 0][None] * values, axis=1)
    flat_state = flat_state.at[:, ghost_cell[0, 0, 0]].set(ghost_value)
    filled = flat_state.reshape(4, cells_x, cells_y, cells_z)
    span_index = lax.axis_index("gy")
    total_span = lax.axis_size("gy") * cells_y
    tile_list = near_tiles[0, 0, 0]
    cell_list = cell_coords(tile_list, span_index * cells_y, total_span, cells_x, cells_y, cells_z)
    points = rotate(surface[0, 0], pitch_angle)
    initial = jnp.full((tile_list.shape[0], TY * cells_z), jnp.inf, jnp.float32)
    nearest_sq = closest(cell_list, lax.all_gather(points, "gy", axis=1, tiled=True), initial)
    distance = jnp.minimum(jnp.sqrt(nearest_sq + dist_eps), dist_cap)
    wall_distance = place_tiles(tile_list, distance, cells_x, cells_y, cells_z)
    padded = with_halo(filled, (("gx", 1), ("gy", 2), ("gz", 3)), 2)
    new_velocity, new_nu_tilde = advance(padded, wall_distance, fluid_cells)
    return (new_velocity, new_nu_tilde, wall_distance)


def solution(mesh):
    in_specs = (
        P(None, "gx", "gy", "gz"),
        P("gx", "gy", "gz"),
        P("gx", "gy", "gz"),
        P("gx", "gz", None, "gy"),
        P(),
        P("gx", "gy", "gz", None),
        P("gx", "gy", "gz", None, None),
        P("gx", "gy", "gz", None),
        P("gx", "gy", "gz", None, None),
        P("gx", "gy", "gz", None, None),
    )
    out_specs = (P(None, "gx", "gy", "gz"), P("gx", "gy", "gz"), P("gx", "gy", "gz"))
    return jax.shard_map(
        on_device, mesh=mesh, in_specs=in_specs, out_specs=out_specs, check_vma=False
    )
```

profile of v0, /device:TPU:0, one launch (start us, length us, event | category | flops | bytes accessed | tf_op | source)
XLA Modules:
  0.0 220.2 jit_solution(13812162060099592031)
XLA Ops:
  0.6 0.7 fusion.51
  1.3 0.7 compare_bitcast_fusion
  2.0 1.3 copy.70
  3.3 1.1 pad_maximum_fusion.14
  4.4 0.0 copy-start.12
  4.5 0.0 copy-start.13
  4.5 8.6 %copy.50 = f32[4,32768]{0,1:T(8,128)} copy(f32[4,32768]{1,0:T(4,128)S(1)} %pad_maximum_fusion.14) | data formatting | bytes 1048576 | tf_op jit(solution)/shard_map/concatenate | solution.py:153
  13.1 8.6 %gather_fusion = f32[1024,4]{1,0:T(8,128)S(1)} fusion(f32[4,32768]{0,1:T(8,128)} %copy.50, s32[1024]{0:T(1024)S(1)} %fusion.51), kind=kCustom, calls=%fused_computation | custom fusion | bytes 36864 | tf_op jit(solution)/shard_map/gather | solution.py:157
  21.6 0.2 copy.48
  21.8 0.6 select_bitcast_fusion
  22.5 6.3 %all-to-all-start = ((f32[4,8,128]{2,0,1:T(4,128)}), f32[4,8,128]{2,0,1:T(4,128)S(1)}, u32[]{:S(2)}, u32[]{:S(2)}) async-start(f32[4,8,128]{2,0,1:T(4,128)} %select_bitcast_fusion), calls=%async_computation | async-start | bytes 32768 | tf_op jit(solution)/shard_map/all_to_all | solution.py:158
  29.7 8.1 %all_gather.3 = f32[3,512]{1,0:T(4,128)S(1)} all-gather(f32[3,128]{1,0:T(4,128)S(1)} %pad_maximum_fusion.19), channel_id=1, replica_groups=mesh['gx'=2,'gy'=4,'gz'=4] {'gy'}, dimensions={1}, use_global_device_ids=true | all-gather | bytes 7680 | tf_op jit(solution)/shard_map/all_gather | solution.py:170
  37.9 0.1 convert_add_fusion
  37.9 0.1 stack_broadcast_in_dim.7
  38.0 0.1 stack_broadcast_in_dim.6
  38.1 8.6 %while.10 = (s32[]{:T(128)}, f32[8,1024]{1,0:T(8,128)S(1)}, f32[8,3,1024]{2,0,1:T(8,128)S(1)}, f32[3,512]{1,0:T(4,128)S(1)}, s32[]{:T(128)}, /*index=5*/s32[]{:T(128)}, s32[]{}, s32[]{}) while((s32[]{:T(128)}, f32[8,1024]{1,0:T(8,128)S(1)}, f32[8,3,1024]{2,0,1:T(8,128)S(1)}, f32[3,512]{1,0:T(4,128)S(1)}, s32[]{:T(128)}, /*index=5*/s32[]{:T(128)}, ...), condition=%wide.region_4.5_spmd, body=%wide.region_2.4_spmd.sunk | while | flops 4717572 | bytes 67709 | solution.py:72
  38.2 0.9 add_reduce_fusion.2
  39.1 0.1 dynamic_update_slice.5
  39.3 0.9 add_reduce_fusion.2
  40.2 0.1 dynamic_update_slice.5
  40.3 0.9 add_reduce_fusion.2
  41.2 0.1 dynamic_update_slice.5
  41.4 0.9 add_reduce_fusion.2
  42.3 0.1 dynamic_update_slice.5
  42.5 0.9 add_reduce_fusion.2
  43.4 0.1 dynamic_update_slice.5
  43.5 0.9 add_reduce_fusion.2
  44.4 0.1 dynamic_update_slice.5
  44.6 0.9 add_reduce_fusion.2
  45.5 0.1 dynamic_update_slice.5
  45.7 0.9 add_reduce_fusion.2
  46.6 0.1 dynamic_update_slice.5
  46.7 0.7 scatter_custom_fusion.1
  47.4 0.7 reshape.295
  48.1 0.2 copy.49
  48.3 54.8 %gather_fusion.1 = f32[16384,4]{1,0:T(8,128)} fusion(f32[4,1024]{0,1:T(8,128)S(1)} %bitcast.129, s32[16384]{0:T(1024)S(1)} %broadcast_clamp_fusion), kind=kCustom, calls=%fused_computation.1 | custom fusion | bytes 589824 | tf_op jit(solution)/shard_map/gather | solution.py:160
  103.1 5.3 %multiply_reduce_fusion = f32[2048,4]{1,0:T(8,128)S(1)} fusion(f32[8,2048,4]{2,1,0:T(8,128)} %bitcast.130, f32[8,2048]{1,0:T(8,128)S(1)} %bitcast.148), kind=kLoop, calls=%fused_computation.15 | loop fusion | flops 122880 | bytes 360448 | tf_op jit(solution)/shard_map/reduce_sum | solution.py:161
  108.4 17.1 %scatter_custom_fusion = f32[4,32768]{0,1:T(8,128)} fusion(f32[4,32768]{0,1:T(8,128)} %copy.50, s32[2048]{0:T(1024)S(1)} %bitcast.149, f32[2048,4]{1,0:T(8,128)S(1)} %multiply_reduce_fusion), kind=kCustom, calls=%fused_computation.16 | custom fusion | flops 8192 | bytes 1572864 | tf_op jit(solution)/shard_map/scatter | solution.py:162
  125.5 10.0 %copy.51 = f32[4,8,32,128]{3,2,1,0:T(8,128)S(1)} copy(f32[4,8,32,128]{0,3,2,1:T(8,128)} %bitcast.127) | data formatting | bytes 1048576 | tf_op jit(solution)/shard_map/reshape | solution.py:163
  135.6 1.3 collective-permute-start
  136.9 1.5 collective-permute-start.1
  138.3 42.3 %slice_reduce_fusion = (f32[32768]{0:T(1024)}, f32[32768]{0:T(1024)}, f32[32768]{0:T(1024)}, f32[32768]{0:T(1024)}) fusion(f32[4,32768]{0,1:T(8,128)} %scatter_custom_fusion), kind=kLoop, calls=%fused_computation.8 | loop fusion | flops 98304 | bytes 1048576 | tf_op jit(solution)/shard_map/slice | solution.py:104
  180.6 10.6 %copy.61 = f32[3,8,32,128]{3,2,1,0:T(8,128)} copy(f32[3,8,32,128]{0,3,2,1:T(8,128)} %bitcast.128) | data formatting | bytes 786432 | tf_op jit(solution)/shard_map/slice | solution.py:103
  191.3 3.4 %collective-permute-start.2 = (f32[4,12,2,128]{3,2,1,0:T(2,128)S(1)}, f32[4,12,2,128]{3,2,1,0:T(2,128)S(1)}, u32[]{:S(2)}, u32[]{:S(2)}) collective-permute-start(f32[4,12,2,128]{3,2,1,0:T(2,128)S(1)} %get-tuple-element.67), channel_id=1, source_target_pairs={{0,4},{4,8},{8,12},{1,5},{5,9},{9,13},{2,6},{6,10},{10,14},{3,7},{... | collective-permute-start | bytes 147464 | tf_op jit(solution)/shard_map/ppermute | solution.py:28
  194.7 1.3 collective-permute-start.3
  196.0 1.2 broadcast_multiply_fusion.2
  197.2 3.9 %collective-permute-done.3 = f32[4,12,2,128]{3,2,1,0:T(2,128)S(1)} collective-permute-done((f32[4,12,2,128]{3,2,1,0:T(2,128)S(1)}, f32[4,12,2,128]{3,2,1,0:T(2,128)S(1)}, u32[]{:S(2)}, u32[]{:S(2)}) %collective-permute-start.3) | collective-permute-done | bytes 49184 | tf_op jit(solution)/shard_map/ppermute | solution.py:31
  201.1 0.1 pad_maximum_fusion.1
  201.2 0.3 fusion.60
  201.6 0.4 copy.56
  202.0 3.9 %collective-permute-start.4 = (f32[4,12,36,2]{2,0,3,1:T(4,128)S(1)}, f32[4,12,36,2]{2,0,3,1:T(4,128)S(1)}, u32[]{:S(2)}, u32[]{:S(2)}) collective-permute-start(f32[4,12,36,2]{2,0,3,1:T(4,128)S(1)} %copy.56), channel_id=1, source_target_pairs={{0,1},{1,2},{2,3},{4,5},{5,6},{6,7},{8,9},{9,10},{10,11},{12,13},{... | collective-permute-start | bytes 41480 | tf_op jit(solution)/shard_map/ppermute | solution.py:28
  205.9 0.4 copy.58
  206.4 1.3 collective-permute-start.5
  207.7 0.2 pad_maximum_fusion
  207.8 1.3 broadcast_multiply_fusion.1
  209.1 0.5 copy.57
  209.6 2.8 %collective-permute-done.5 = f32[4,12,36,2]{2,0,3,1:T(4,128)} collective-permute-done((f32[4,12,36,2]{2,0,3,1:T(4,128)S(1)}, f32[4,12,36,2]{2,0,3,1:T(4,128)}, u32[]{:S(2)}, u32[]{:S(2)}) %collective-permute-start.5) | collective-permute-done | bytes 13856 | tf_op jit(solution)/shard_map/ppermute | solution.py:31
  212.4 1.3 copy.59
  213.7 0.0 copy-start.8
  213.8 1.2 broadcast_multiply_fusion
  214.9 1.5 multiply_add_fusion
  216.5 1.8 subtract_add_fusion
  218.3 1.0 fusion.38
  219.3 0.9 fusion.13
  (64 shorter events, 0.5 us)
Async XLA Ops:
  4.4 25.2 %copy-start.11 = (s32[1,1,1,8,2048]{4,3,2,1,0:T(8,128)S(1)}, s32[1,1,1,8,2048]{4,3,2,1,0:T(8,128)}, u32[]{:S(2)}) copy-start(s32[1,1,1,8,2048]{4,3,2,1,0:T(8,128)} %param.20) | copy-start | bytes 196612
  4.4 25.2 %copy-start.12 = (s32[1,1,1,2048]{3,2,1,0:T(1,128)S(1)}, s32[1,1,1,2048]{3,2,1,0:T(1,128)}, u32[]{:S(2)}) copy-start(s32[1,1,1,2048]{3,2,1,0:T(1,128)} %param.19) | copy-start | bytes 24580
  4.5 25.3 %copy-start.13 = (f32[1,1,3,128]{3,1,2,0:T(1,128)S(1)}, f32[1,1,3,128]{3,1,2,0:T(1,128)}, u32[]{:S(2)}) copy-start(f32[1,1,3,128]{3,1,2,0:T(1,128)} %param.15) | copy-start | bytes 4612
  4.5 33.4 %copy-start.14 = (s32[1,1,1,8]{3,2,1,0:T(1,128)S(1)}, s32[1,1,1,8]{3,2,1,0:T(1,128)}, u32[]{:S(2)}) copy-start(s32[1,1,1,8]{3,2,1,0:T(1,128)} %param.17) | copy-start | bytes 100
  4.5 98.7 %copy-start.10 = (f32[1,1,1,8,2048]{4,3,2,1,0:T(8,128)S(1)}, f32[1,1,1,8,2048]{4,3,2,1,0:T(8,128)}, u32[]{:S(2)}) copy-start(f32[1,1,1,8,2048]{4,3,2,1,0:T(8,128)} %param.21) | copy-start | bytes 196612
  22.5 25.6 %all-to-all-start = ((f32[4,8,128]{2,0,1:T(4,128)}), f32[4,8,128]{2,0,1:T(4,128)S(1)}, u32[]{:S(2)}, u32[]{:S(2)}) async-start(f32[4,8,128]{2,0,1:T(4,128)} %select_bitcast_fusion), calls=%async_computation | async-start | bytes 32768 | tf_op jit(solution)/shard_map/all_to_all | solution.py:158
  135.6 55.7 %collective-permute-start = (f32[4,2,32,128]{3,2,1,0:T(8,128)S(1)}, f32[4,2,32,128]{3,2,1,0:T(8,128)S(1)}, u32[]{:S(2)}, u32[]{:S(2)}) collective-permute-start(f32[4,2,32,128]{3,2,1,0:T(8,128)S(1)} %get-tuple-element.68), channel_id=1, source_target_pairs={{0,16},{1,17},{2,18},{3,19},{4,20},{5,21},{6,22},{7,23},{8,24},{9,... | collective-permute-start | bytes 393224 | tf_op jit(solution)/shard_map/ppermute | solution.py:28
  136.9 54.4 %collective-permute-start.1 = (f32[4,2,32,128]{3,2,1,0:T(8,128)S(1)}, f32[4,2,32,128]{3,2,1,0:T(8,128)S(1)}, u32[]{:S(2)}, u32[]{:S(2)}) collective-permute-start(f32[4,2,32,128]{3,2,1,0:T(8,128)S(1)} %get-tuple-element.69), channel_id=1, source_target_pairs={{16,0},{17,1},{18,2},{19,3},{20,4},{21,5},{22,6},{23,7},{24,8},{25... | collective-permute-start | bytes 393224 | tf_op jit(solution)/shard_map/ppermute | solution.py:31
  191.2 17.9 %copy-start.1 = (f32[4,2,32,128]{3,2,1,0:T(8,128)}, f32[4,2,32,128]{3,2,1,0:T(8,128)S(1)}, u32[]{:S(2)}) copy-start(f32[4,2,32,128]{3,2,1,0:T(8,128)S(1)} %collective-permute-done) | copy-start | bytes 393220
  191.2 17.9 %copy-start.2 = (f32[4,2,32,128]{3,2,1,0:T(8,128)}, f32[4,2,32,128]{3,2,1,0:T(8,128)S(1)}, u32[]{:S(2)}) copy-start(f32[4,2,32,128]{3,2,1,0:T(8,128)S(1)} %collective-permute-done.1) | copy-start | bytes 393220
  191.3 5.9 %collective-permute-start.2 = (f32[4,12,2,128]{3,2,1,0:T(2,128)S(1)}, f32[4,12,2,128]{3,2,1,0:T(2,128)S(1)}, u32[]{:S(2)}, u32[]{:S(2)}) collective-permute-start(f32[4,12,2,128]{3,2,1,0:T(2,128)S(1)} %get-tuple-element.67), channel_id=1, source_target_pairs={{0,4},{4,8},{8,12},{1,5},{5,9},{9,13},{2,6},{6,10},{10,14},{3,7},{... | collective-permute-start | bytes 147464 | tf_op jit(solution)/shard_map/ppermute | solution.py:28
  194.7 6.4 %collective-permute-start.3 = (f32[4,12,2,128]{3,2,1,0:T(2,128)S(1)}, f32[4,12,2,128]{3,2,1,0:T(2,128)S(1)}, u32[]{:S(2)}, u32[]{:S(2)}) collective-permute-start(f32[4,12,2,128]{3,2,1,0:T(2,128)S(1)} %get-tuple-element.66), channel_id=1, source_target_pairs={{4,0},{8,4},{12,8},{5,1},{9,5},{13,9},{6,2},{10,6},{14,10},{7,3},{... | collective-permute-start | bytes 147464 | tf_op jit(solution)/shard_map/ppermute | solution.py:31
  201.1 8.5 %copy-start.6 = (f32[4,12,2,128]{3,2,1,0:T(2,128)}, f32[4,12,2,128]{3,2,1,0:T(2,128)S(1)}, u32[]{:S(2)}) copy-start(f32[4,12,2,128]{3,2,1,0:T(2,128)S(1)} %collective-permute-done.3) | copy-start | bytes 147460
  202.0 7.1 %collective-permute-start.4 = (f32[4,12,36,2]{2,0,3,1:T(4,128)S(1)}, f32[4,12,36,2]{2,0,3,1:T(4,128)S(1)}, u32[]{:S(2)}, u32[]{:S(2)}) collective-permute-start(f32[4,12,36,2]{2,0,3,1:T(4,128)S(1)} %copy.56), channel_id=1, source_target_pairs={{0,1},{1,2},{2,3},{4,5},{5,6},{6,7},{8,9},{9,10},{10,11},{12,13},{... | collective-permute-start | bytes 41480 | tf_op jit(solution)/shard_map/ppermute | solution.py:28
  206.4 6.1 %collective-permute-start.5 = (f32[4,12,36,2]{2,0,3,1:T(4,128)S(1)}, f32[4,12,36,2]{2,0,3,1:T(4,128)}, u32[]{:S(2)}, u32[]{:S(2)}) collective-permute-start(f32[4,12,36,2]{2,0,3,1:T(4,128)S(1)} %copy.58), channel_id=1, source_target_pairs={{1,0},{2,1},{3,2},{5,4},{6,5},{7,6},{9,8},{10,9},{11,10},{13,12},{... | collective-permute-start | bytes 41480 | tf_op jit(solution)/shard_map/ppermute | solution.py:31
  207.8 1.3 copy-start
  213.7 4.6 %copy-start.3 = (f32[4,8,32,128]{3,2,1,0:T(8,128)S(1)}, f32[4,8,32,128]{3,2,1,0:T(8,128)}, u32[]{:S(2)}) copy-start(f32[4,8,32,128]{3,2,1,0:T(8,128)} %get-tuple-element.50) | copy-start | bytes 1572868
  213.7 4.6 %copy-start.4 = (f32[4,8,32,128]{3,2,1,0:T(8,128)S(1)}, f32[4,8,32,128]{3,2,1,0:T(8,128)}, u32[]{:S(2)}) copy-start(f32[4,8,32,128]{3,2,1,0:T(8,128)} %get-tuple-element.52) | copy-start | bytes 1572868
  213.7 4.6 %copy-start.7 = (f32[32768]{0:T(1024)S(1)}, f32[32768]{0:T(1024)}, u32[]{:S(2)}) copy-start(f32[32768]{0:T(1024)} %get-tuple-element.38) | copy-start | bytes 393220
  213.7 4.6 %copy-start.8 = (f32[8,32,128]{2,1,0:T(8,128)S(1)}, f32[8,32,128]{2,1,0:T(8,128)}, u32[]{:S(2)}) copy-start(f32[8,32,128]{2,1,0:T(8,128)} %reshape.295) | copy-start | bytes 393220
  213.7 4.6 %copy-start.9 = (s32[8,32,128]{2,1,0:T(8,128)S(1)}, s32[8,32,128]{2,1,0:T(8,128)}, u32[]{:S(2)}) copy-start(s32[8,32,128]{2,1,0:T(8,128)} %param.14) | copy-start | bytes 393220
  213.7 5.5 %copy-start.5 = (f32[3,8,32,128]{3,2,1,0:T(8,128)S(1)}, f32[3,8,32,128]{3,2,1,0:T(8,128)}, u32[]{:S(2)}) copy-start(f32[3,8,32,128]{3,2,1,0:T(8,128)} %copy.61) | copy-start | bytes 1179652
where the time goes:
time: 221 us; the launch traced here: 220 us
  local copies, waits for them, and re-layouts  99.2 us (45%)
  other arithmetic  84.9 us (38%)
  starting transfers between devices  19 us (9%)
  blocking collectives  8.07 us (4%)
  waiting for transfers between devices  6.76 us (3%)
    gather x1, local copies, waits for them, and re-layouts, on_device(): values = buffer[:, ghost_src[0, 0, 0]]  54.8 us
    slice x1, other arithmetic, advance(): working = center[3]  42.3 us
    scatter x1, other arithmetic, on_device(): flat_state = flat_state.at[:, ghost_cell[0, 0, 0]].set(ghost_value)  17.1 us
    slice x1, local copies, waits for them, and re-layouts, advance(): moving = center[:3]  10.6 us
    reshape x1, local copies, waits for them, and re-layouts, on_device(): filled = flat_state.reshape(4, cells_x, cells_y, cells_z)  10 us
    gather x2, local copies, waits for them, and re-layouts, on_device(): flat_state[:, jnp.where(live_rows, row_list, 0)]  8.76 us
    ppermute x3, starting transfers between devices, with_halo(): lax.ppermute(lax.slice_in_dim(block, block.shape[dim] - width, None, axis...  8.62 us
    concatenate x1, local copies, waits for them, and re-layouts, on_device(): fields = jnp.concatenate([velocity, nu_tilde[None]], axis=0)  8.57 us
  transfers between devices with their start and end apart: 7, of which 2 were waited for; matrix products, arithmetic and copies ran while one was open for 30% of the time, Pallas kernels for 0%

commit v1 on v0

v1 whole, which is shorter than its diff:
```python
import functools

import jax
import jax.numpy as jnp
from jax import lax
from jax.experimental import pallas as pl
from jax.experimental.pallas import tpu as pltpu
from jax.sharding import PartitionSpec as P

MESH = pl.DeviceIdType.MESH
TY = 8
LANES = 128

viscosity = 0.2
prod_coef = 0.1355
grad_coef = 0.622
sigma_inv = 1.5
karman = 0.41
visc_coef = 7.1
wall_coef = prod_coef / (karman * karman) + (1.0 + grad_coef) * sigma_inv
des_coef = 0.65
floor_rate = 0.3
dist_eps = 0.25
dist_cap = 8.0
time_step = 0.05


def lookup(row, lanes):
    table = jnp.broadcast_to(row, lanes.shape)
    return jnp.take_along_axis(table, lanes, axis=1, mode="promise_in_bounds")


def step_kernel(
    sizes,
    vel_ref,
    nu_ref,
    fluid_ref,
    surf_ref,
    pitch_ref,
    tiles_ref,
    rows_ref,
    cell_ref,
    src_ref,
    weight_ref,
    new_vel_ref,
    new_nu_ref,
    wall_ref,
    out_buf,
    in_buf,
    points,
    inverse,
    ghost,
    padded,
    edge_z,
    turn,
    pack_y,
    got_y,
    pack_z,
    got_z,
    flat_x,
    flat_y,
    flat_z2,
    dist,
    peer_send,
    peer_recv,
    point_send,
    point_recv,
    halo_send,
    halo_recv,
):
    nx, ny, nz = sizes
    peers = nx * nz
    _, cx, cy, cz = vel_ref.shape
    rows_y = cy // 8
    chunks = cell_ref.shape[1] // LANES
    a, b, c = (lax.axis_index(name) for name in ("gx", "gy", "gz"))
    me = a * nz + c
    slots = tiles_ref.shape[0]
    per_row = cy // TY
    lane = lax.broadcasted_iota(jnp.int32, (8, LANES), 1)

    def field(f, i, start, count):
        if f < 3:
            return vel_ref[f, i, pl.ds(start, count), :]
        return nu_ref[i, pl.ds(start, count), :]

    def peer_of(d):
        other = lax.rem(me + d, peers)
        return other, (lax.div(other, nz), b, lax.rem(other, nz))

    def column_of(d):
        other = lax.rem(b + d, ny)
        return other, (a, other, c)

    barrier = pltpu.get_barrier_semaphore()
    for d in range(1, peers):
        pl.semaphore_signal(barrier, inc=1, device_id=peer_of(d)[1], device_id_type=MESH)
    for d in range(1, ny):
        pl.semaphore_signal(barrier, inc=1, device_id=column_of(d)[1], device_id_type=MESH)

    angle = jnp.full((1, LANES), pitch_ref[0], jnp.float32)
    cosine, sine = jnp.cos(angle), jnp.sin(angle)
    px, py, pz = surf_ref[0:1, :], surf_ref[1:2, :], surf_ref[2:3, :]
    points[b] = jnp.concatenate(
        [cosine * px + sine * pz, py, cosine * pz - sine * px, jnp.zeros((5, LANES), jnp.float32)], axis=0
    )

    groups = peers // 8
    listed = [rows_ref[8 * g : 8 * g + 8, :] for g in range(groups)]
    listed_row = [lax.shift_right_arithmetic(x, 7) for x in listed]
    listed_lane = [x & (LANES - 1) for x in listed]

    def pick(i, acc):
        acc = list(acc)
        for j in range(cy):
            for g in range(groups):
                here = listed_row[g] == i * cy + j
                for f in range(4):
                    found = lookup(field(f, i, j, 1), listed_lane[g])
                    acc[4 * g + f] = jnp.where(here, found, acc[4 * g + f])
        return tuple(acc)

    picked = lax.fori_loop(0, cx, pick, tuple(jnp.zeros((8, LANES), jnp.float32) for _ in range(4 * groups)))
    for g in range(groups):
        for r in range(8):
            for f in range(4):
                out_buf[8 * g + r, f : f + 1, :] = picked[4 * g + f][r : r + 1, :]

    pl.semaphore_wait(barrier, peers - 1 + ny - 1)

    def peer_copy(d):
        other, device = peer_of(d)
        return pltpu.make_async_remote_copy(
            src_ref=out_buf.at[other],
            dst_ref=in_buf.at[me],
            send_sem=peer_send.at[d],
            recv_sem=peer_recv.at[d],
            device_id=device,
            device_id_type=MESH,
        )

    def point_copy(d):
        return pltpu.make_async_remote_copy(
            src_ref=points.at[b],
            dst_ref=points.at[b],
            send_sem=point_send.at[d],
            recv_sem=point_recv.at[d],
            device_id=column_of(d)[1],
            device_id_type=MESH,
        )

    peer_copies = [peer_copy(d) for d in range(1, peers)]
    for copy in peer_copies:
        copy.start()
    point_copies = [point_copy(d) for d in range(1, ny)]
    for copy in point_copies:
        copy.start()
    in_buf[me] = out_buf[me]

    def invert(pair, total):
        cells = cell_ref[:, pl.ds(pl.multiple_of(pair * 256, 256), 256)]
        at_row = lax.shift_right_arithmetic(cells, 7)
        at_lane = cells & (LANES - 1)
        row_id = lax.broadcasted_iota(jnp.int32, (cx * cy, 256), 0)
        lane_id = lax.broadcasted_iota(jnp.int32, (LANES, 256), 0)
        number = lax.broadcasted_iota(jnp.int32, (LANES, 256), 1) + pair * 256
        chunk_id = (lax.shift_right_arithmetic(number, 7) + 1).astype(jnp.float32)
        place = (number & (LANES - 1)).astype(jnp.float32)
        hit_row = jnp.where(row_id == at_row, 1.0, 0.0).astype(jnp.bfloat16)
        hit_lane = lane_id == at_lane
        code = jnp.concatenate(
            [jnp.where(hit_lane, chunk_id, 0.0), jnp.where(hit_lane, place, 0.0)], axis=0
        ).astype(jnp.bfloat16)
        return total + lax.dot_general(
            hit_row, code, (((1,), (1,)), ((), ())), preferred_element_type=jnp.float32
        )

    inverse[...] = lax.fori_loop(
        0, chunks // 2, invert, jnp.zeros((cx * cy, 2 * LANES), jnp.float32)
    ).astype(jnp.int32).reshape(cx, cy, 2 * LANES)

    for copy in peer_copies:
        copy.wait_recv()

    def interpolate(m, carry):
        at = pl.ds(pl.multiple_of(m * LANES, LANES), LANES)
        source = src_ref[:, at]
        weight = weight_ref[:, at]
        from_peer = lax.shift_right_arithmetic(source, 7)
        from_slot = source & (LANES - 1)

        def one_peer(p, acc):
            here = from_peer == p
            return tuple(
                jnp.where(here, lookup(in_buf[p, f : f + 1, :], from_slot), acc[f]) for f in range(4)
            )

        acc = tuple(jnp.zeros((8, LANES), jnp.float32) for _ in range(4))
        if peers <= 8:
            for p in range(peers):
                acc = one_peer(p, acc)
        else:
            acc = lax.fori_loop(0, peers, one_peer, acc)
        for f in range(4):
            ghost[f, pl.ds(m, 1), :] = -jnp.sum(weight * acc[f], axis=0, keepdims=True)
        return carry

    lax.fori_loop(0, chunks, interpolate, 0)

    def fill(i, carry):
        for jb in range(rows_y):
            chunk_id = inverse[i, 8 * jb : 8 * jb + 8, 0:LANES]
            place = inverse[i, 8 * jb : 8 * jb + 8, LANES : 2 * LANES]
            value = [field(f, i, 8 * jb, 8) for f in range(4)]
            for m in range(chunks):
                here = chunk_id == m + 1
                for f in range(4):
                    value[f] = jnp.where(here, lookup(ghost[f, m : m + 1, :], place), value[f])
            for f in range(4):
                padded[f, i + 2, 8 + 8 * jb : 16 + 8 * jb, :] = value[f]
        return carry

    low_high = ((a, nx), (b, ny), (c, nz))

    def exists(axis, side):
        index, count = low_high[axis]
        return index > 0 if side == 0 else index < count - 1

    def beside(axis, side):
        place = [a, b, c]
        place[axis] = place[axis] + (1 if side else -1)
        return tuple(place)

    def halo_copy(axis, side):
        if axis == 0:
            source = padded.at[:, 2:4, 8 : 8 + cy, :] if side == 0 else padded.at[:, cx : cx + 2, 8 : 8 + cy, :]
            target = padded.at[:, cx + 2 : cx + 4, 8 : 8 + cy, :] if side == 0 else padded.at[:, 0:2, 8 : 8 + cy, :]
        else:
            pack, got = ((pack_y, got_y), (pack_z, got_z))[axis - 1]
            source, target = pack.at[side], got.at[1 - side]
        return pltpu.make_async_remote_copy(
            src_ref=source,
            dst_ref=target,
            send_sem=halo_send.at[2 * axis + side],
            recv_sem=halo_recv.at[2 * axis + 1 - side],
            device_id=beside(axis, side),
            device_id_type=MESH,
        )

    def send_halo(axis):
        for side in range(2):
            @pl.when(exists(axis, side))
            def _():
                halo_copy(axis, side).start()

    def wait_halo(axis):
        for side in range(2):
            @pl.when(exists(axis, side))
            def _():
                pltpu.make_async_remote_copy(
                    src_ref=halo_source(axis, side),
                    dst_ref=halo_target(axis, side),
                    send_sem=halo_send.at[2 * axis + side],
                    recv_sem=halo_recv.at[2 * axis + side],
                    device_id=beside(axis, side),
                    device_id_type=MESH,
                ).wait_recv()

    def halo_source(axis, side):
        if axis == 0:
            return padded.at[:, 2:4, 8 : 8 + cy, :] if side == 0 else padded.at[:, cx : cx + 2, 8 : 8 + cy, :]
        return (pack_y, pack_z)[axis - 1].at[side]

    def halo_target(axis, side):
        if axis == 0:
            return padded.at[:, 0:2, 8 : 8 + cy, :] if side == 0 else padded.at[:, cx + 2 : cx + 4, 8 : 8 + cy, :]
        return (got_y, got_z)[axis - 1].at[side]

    lax.fori_loop(0, 2, fill, 0)
    lax.fori_loop(cx - 2, cx, fill, 0)
    send_halo(0)
    lax.fori_loop(2, cx - 2, fill, 0)
    for f in range(4):
        for i in range(cx):
            at = 2 * (f * cx + i)
            pack_y[0, at : at + 2, :] = padded[f, i + 2, 8:10, :]
            pack_y[1, at : at + 2, :] = padded[f, i + 2, 6 + cy : 8 + cy, :]
    send_halo(1)
    planes = LANES // cy
    blocks = cx // planes
    for f in range(4):
        for g in range(blocks):
            block = padded[f, 2 + planes * g : 2 + planes * (g + 1), 8 : 8 + cy, :].reshape(LANES, LANES)
            across = block.T
            at = 2 * (f * blocks + g)
            pack_z[0, at : at + 2, :] = across[0:2, :]
            pack_z[1, at : at + 2, :] = across[LANES - 2 : LANES, :]
    send_halo(2)

    for side in range(2):
        @pl.when(jnp.logical_not(exists(0, side)))
        def _():
            begin = 0 if side == 0 else cx + 2
            padded[:, begin : begin + 2, 8 : 8 + cy, :] = jnp.zeros((4, 2, cy, LANES), jnp.float32)

        @pl.when(jnp.logical_not(exists(1, side)))
        def _():
            got_y[side] = jnp.zeros(got_y.shape[1:], jnp.float32)

        @pl.when(jnp.logical_not(exists(2, side)))
        def _():
            got_z[side] = jnp.zeros(got_z.shape[1:], jnp.float32)

    for copy in point_copies:
        copy.wait_recv()
    deep = (lax.broadcasted_iota(jnp.int32, (LANES, LANES), 1).astype(jnp.float32) + 0.5) - 0.5 * cz
    for g in range(ny):
        at = slice(LANES * g, LANES * (g + 1))
        flat_x[at, :] = jnp.broadcast_to(points[g, 0:1, :], (LANES, LANES)).T
        flat_y[at, :] = jnp.broadcast_to(points[g, 1:2, :], (LANES, LANES)).T
        step_z = deep - jnp.broadcast_to(points[g, 2:3, :], (LANES, LANES)).T
        flat_z2[at, :] = step_z * step_z

    def one_slot(s, carry):
        tile = jnp.maximum(tiles_ref[s], 0)
        plane = lax.div(tile, per_row).astype(jnp.float32)
        first = lax.rem(tile, per_row) * TY + b * cy
        at_x = jnp.full((8, LANES), plane + 0.5 - 0.5 * cx, jnp.float32)
        at_y = [
            jnp.full((8, LANES), (first + r).astype(jnp.float32) + 0.5 - 0.5 * (ny * cy), jnp.float32)
            for r in range(TY)
        ]

        def some_points(k, best):
            for u in range(4):
                at = pl.ds(pl.multiple_of(k * 32, 32) + 8 * u, 8)
                step_x = at_x - flat_x[at, :]
                both = step_x * step_x + flat_z2[at, :]
                beside_y = flat_y[at, :]
                new = []
                for r in range(TY):
                    step_y = at_y[r] - beside_y
                    new.append(jnp.minimum(best[r], step_y * step_y + both))
                best = tuple(new)
            return best

        start = tuple(jnp.full((8, LANES), jnp.inf, jnp.float32) for _ in range(TY))
        best = lax.fori_loop(0, ny * LANES // 32, some_points, start)
        least = jnp.concatenate([jnp.min(x, axis=0, keepdims=True) for x in best], axis=0)
        dist[s] = jnp.minimum(jnp.sqrt(least + dist_eps), dist_cap)
        return carry

    lax.fori_loop(0, slots, one_slot, 0)

    for axis in range(3):
        wait_halo(axis)
    for f in range(4):
        for i in range(cx):
            at = 2 * (f * cx + i)
            padded[f, i + 2, 6:8, :] = got_y[0, at : at + 2, :]
            padded[f, i + 2, 8 + cy : 10 + cy, :] = got_y[1, at : at + 2, :]
    turn[...] = jnp.zeros(turn.shape, jnp.float32)
    for f in range(4):
        for g in range(blocks):
            at = 2 * (f * blocks + g)
            turn[0:2, :] = got_z[1, at : at + 2, :]
            turn[LANES - 2 : LANES, :] = got_z[0, at : at + 2, :]
            edge_z[f, planes * g : planes * (g + 1), :, :] = turn[...].T.reshape(planes, cy, LANES)

    def advance(i, carry):
        for jb in range(rows_y):
            advance_rows(i, jb)
        return carry

    def advance_rows(i, jb):
        center, gradient, laplace = [], [[], [], []], []

        def slope(m2, m1, p1, p2):
            return ((m2 - p2) + 8.0 * (p1 - m1)) * (1.0 / 12.0)

        for f in range(4):
            begin = 8 + 8 * jb
            mid = padded[f, i + 2, begin : begin + 8, :]
            x = [padded[f, i + 2 + h, begin : begin + 8, :] for h in (-2, -1, 1, 2)]
            y = [padded[f, i + 2, begin + h : begin + h + 8, :] for h in (-2, -1, 1, 2)]
            rim = edge_z[f, i, 8 * jb : 8 * jb + 8, :]
            z = [
                pltpu.roll(jnp.where(lane >= LANES - 2, rim, mid), 2, 1),
                pltpu.roll(jnp.where(lane >= LANES - 1, rim, mid), 1, 1),
                pltpu.roll(jnp.where(lane < 1, rim, mid), LANES - 1, 1),
                pltpu.roll(jnp.where(lane < 2, rim, mid), LANES - 2, 1),
            ]
            center.append(mid)
            for e, line in enumerate((x, y, z)):
                gradient[e].append(slope(*line))
            laplace.append(((x[1] + x[2]) + (y[1] + y[2])) + ((z[1] + z[2]) - 6.0 * mid))
        u, v, w, working = center
        curl_x = gradient[1][2] - gradient[2][1]
        curl_y = gradient[2][0] - gradient[0][2]
        curl_z = gradient[0][1] - gradient[1][0]
        rate = jnp.maximum(jnp.sqrt(curl_x * curl_x + curl_y * curl_y + curl_z * curl_z), floor_rate)
        positive = jnp.maximum(working, 0.0)
        chi = positive * (1.0 / viscosity)
        chi_cubed = chi * chi * chi
        diffusion = viscosity + positive * chi_cubed / (chi_cubed + visc_coef**3)
        wall = jnp.full((8, LANES), dist_cap, jnp.float32)
        number = i * per_row + jb
        for s in range(slots):
            wall = jnp.where(tiles_ref[s] == number, dist[s], wall)
        wall_ref[i, 8 * jb : 8 * jb + 8, :] = wall
        arg = (8.0 * diffusion) / (rate * (karman * karman) * (wall * wall))
        shield = 1.0 - jnp.tanh(arg * arg * arg)
        length = wall - shield * jnp.maximum(wall - des_coef, 0.0)
        scale = time_step * fluid_ref[i, 8 * jb : 8 * jb + 8, :].astype(jnp.float32)
        for f in range(4):
            convect = u * gradient[0][f] + v * gradient[1][f] + w * gradient[2][f]
            if f < 3:
                change = diffusion * laplace[f] - convect
                new_vel_ref[f, i, 8 * jb : 8 * jb + 8, :] = center[f] + scale * change
            else:
                squares = (
                    gradient[0][3] * gradient[0][3]
                    + gradient[1][3] * gradient[1][3]
                    + gradient[2][3] * gradient[2][3]
                )
                change = (
                    sigma_inv * ((viscosity + positive) * laplace[3] + grad_coef * squares)
                    - convect
                    + prod_coef * rate * working
                    - wall_coef * working * jnp.abs(working) / (length * length)
                )
                new_nu_ref[i, 8 * jb : 8 * jb + 8, :] = working + scale * change

    lax.fori_loop(0, cx, advance, 0)

    for copy in peer_copies + point_copies:
        copy.wait_send()
    for axis in range(3):
        for side in range(2):
            @pl.when(exists(axis, side))
            def _():
                halo_copy(axis, side).wait_send()


def on_device(
    velocity,
    nu_tilde,
    fluid_cells,
    surface,
    pitch_angle,
    near_tiles,
    send_rows,
    ghost_cell,
    ghost_src,
    ghost_weight,
):
    nx, ny, nz = (lax.axis_size(name) for name in ("gx", "gy", "gz"))
    peers = nx * nz
    _, cx, cy, cz = velocity.shape
    ghosts = ghost_cell.shape[-1]
    points_dev = surface.shape[-1]
    slots = near_tiles.shape[-1]
    vmem = pl.BlockSpec(memory_space=pltpu.VMEM)
    smem = pl.BlockSpec(memory_space=pltpu.SMEM)
    f32 = jnp.float32
    return pl.pallas_call(
        functools.partial(step_kernel, (nx, ny, nz)),
        out_shape=(
            jax.ShapeDtypeStruct(velocity.shape, f32),
            jax.ShapeDtypeStruct(nu_tilde.shape, f32),
            jax.ShapeDtypeStruct(nu_tilde.shape, f32),
        ),
        in_specs=[vmem, vmem, vmem, vmem, smem, smem, vmem, vmem, vmem, vmem],
        out_specs=(vmem, vmem, vmem),
        scratch_shapes=[
            pltpu.VMEM((peers, 4, LANES), f32),
            pltpu.VMEM((peers, 4, LANES), f32),
            pltpu.VMEM((ny, 8, points_dev), f32),
            pltpu.VMEM((cx, cy, 2 * LANES), jnp.int32),
            pltpu.VMEM((4, ghosts // LANES, LANES), f32),
            pltpu.VMEM((4, cx + 4, cy + 16, cz), f32),
            pltpu.VMEM((4, cx, cy, cz), f32),
            pltpu.VMEM((LANES, LANES), f32),
            pltpu.VMEM((2, 8 * cx, cz), f32),
            pltpu.VMEM((2, 8 * cx, cz), f32),
            pltpu.VMEM((2, 8 * cx * cy // LANES, LANES), f32),
            pltpu.VMEM((2, 8 * cx * cy // LANES, LANES), f32),
            pltpu.VMEM((ny * points_dev, cz), f32),
            pltpu.VMEM((ny * points_dev, cz), f32),
            pltpu.VMEM((ny * points_dev, cz), f32),
            pltpu.VMEM((slots, TY, cz), f32),
            pltpu.SemaphoreType.DMA((peers,)),
            pltpu.SemaphoreType.DMA((peers,)),
            pltpu.SemaphoreType.DMA((ny,)),
            pltpu.SemaphoreType.DMA((ny,)),
            pltpu.SemaphoreType.DMA((6,)),
            pltpu.SemaphoreType.DMA((6,)),
        ],
        compiler_params=pltpu.CompilerParams(
            collective_id=0, has_side_effects=True, vmem_limit_bytes=40 * 1024 * 1024
        ),
    )(
        velocity,
        nu_tilde,
        fluid_cells,
        surface[0, 0],
        pitch_angle,
        near_tiles[0, 0, 0],
        send_rows[0, 0, 0],
        ghost_cell[0, 0],
        ghost_src[0, 0, 0],
        ghost_weight[0, 0, 0],
    )


def solution(mesh):
    in_specs = (
        P(None, "gx", "gy", "gz"),
        P("gx", "gy", "gz"),
        P("gx", "gy", "gz"),
        P("gx", "gz", None, "gy"),
        P(),
        P("gx", "gy", "gz", None),
        P("gx", "gy", "gz", None, None),
        P("gx", "gy", "gz", None),
        P("gx", "gy", "gz", None, None),
        P("gx", "gy", "gz", None, None),
    )
    out_specs = (P(None, "gx", "gy", "gz"), P("gx", "gy", "gz"), P("gx", "gy", "gz"))
    return jax.shard_map(
        on_device, mesh=mesh, in_specs=in_specs, out_specs=out_specs, check_vma=False
    )
```

time: 221 us -> 29.6 us (0.13)
  local copies, waits for them, and re-layouts: 99.2 us -> 7.86 us
  other arithmetic: 84.9 us -> 0 us
  Pallas kernels: 0 us -> 20.1 us
  starting transfers between devices: 19 us -> 0 us
  blocking collectives: 8.07 us -> 0 us
  waiting for transfers between devices: 6.76 us -> 0 us
    gather x3 -> x0, local copies, waits for them, and re-layouts: 63.6 us -> none  [the longest x1 54.8 us: on_device(): values = buffer[:, ghost_src[0, 0, 0]]]
    slice x1 -> x0, other arithmetic: 42.3 us -> none  [advance(): working = center[3]]
    pallas_call x0 -> x1, Pallas kernels: none -> 20.1 us  [on_device(): pl.pallas_call(functools.partial(step_kernel, (nx, ny, nz)), out_shape=(j...]
    scatter x2 -> x0, other arithmetic: 17.8 us -> none  [the longest x1 17.1 us: on_device(): flat_state = flat_state.at[:, ghost_cell[0, 0, 0]].set(ghost_value)]
    ppermute x6 -> x0, starting transfers between devices: 12.7 us -> none  [the longest x3 8.62 us: with_halo(): lax.ppermute(lax.slice_in_dim(block, block.shape[dim] - width, None, axis...]
    slice x21 -> x0, local copies, waits for them, and re-layouts: 12.1 us -> none  [the longest x1 10.6 us: advance(): moving = center[:3]]
    reshape x3 -> x0, local copies, waits for them, and re-layouts: 10.7 us -> none  [the longest x1 10 us: on_device(): filled = flat_state.reshape(4, cells_x, cells_y, cells_z)]
    concatenate x1 -> x0, local copies, waits for them, and re-layouts: 8.57 us -> none  [on_device(): fields = jnp.concatenate([velocity, nu_tilde[None]], axis=0)]
  transfers between devices with their start and end apart: 7 -> 0, of which waited for: 2 -> 0; matrix products, arithmetic and copies ran while one was open for 30% -> 0% of each run, Pallas kernels for 0% -> 0%
where the time goes in v1:
time: 29.6 us; the launch traced here: 29.2 us
  Pallas kernels  20.1 us (68%)
  local copies, waits for them, and re-layouts  7.86 us (27%)
  between operations  1.33 us (4%)
    pallas_call x1, Pallas kernels, on_device(): pl.pallas_call(functools.partial(step_kernel, (nx, ny, nz)), out_shape=(j...  20.1 us
    unnamed x22, local copies, waits for them, and re-layouts  7.86 us

profile of v1, /device:TPU:0, one launch (start us, length us, event | category | flops | bytes accessed | tf_op | source)
XLA Modules:
  0.0 29.2 jit_solution(9512439214814035223)
XLA Ops:
  0.6 0.0 copy-start.5
  1.3 0.0 copy-start.8
  1.3 0.0 copy-start.6
  1.3 0.7 %copy-done.8 = f32[1,1,3,128]{3,1,2,0:T(1,128)S(1)} copy-done((f32[1,1,3,128]{3,1,2,0:T(1,128)S(1)}, f32[1,1,3,128]{3,1,2,0:T(1,128)}, u32[]{:S(2)}) %copy-start.8) | copy-done | bytes 1560
  2.0 0.0 copy-start.7
  2.0 0.0 copy-done.5
  2.0 0.0 copy-done.6
  2.0 0.6 %copy-done.7 = s32[1,1,1,8]{3,2,1,0:T(1,128)S(1)} copy-done((s32[1,1,1,8]{3,2,1,0:T(1,128)S(1)}, s32[1,1,1,8]{3,2,1,0:T(1,128)}, u32[]{:S(2)}) %copy-start.7) | copy-done | bytes 56
  2.6 0.0 copy-start
  2.6 1.0 %copy-done = f32[3,8,32,128]{3,2,1,0:T(8,128)S(1)} copy-done((f32[3,8,32,128]{3,2,1,0:T(8,128)S(1)}, f32[3,8,32,128]{3,2,1,0:T(8,128)}, u32[]{:S(2)}) %copy-start) | copy-done | bytes 393240
  3.6 0.0 copy-start.1
  3.6 0.9 %copy-done.1 = f32[8,32,128]{2,1,0:T(8,128)S(1)} copy-done((f32[8,32,128]{2,1,0:T(8,128)S(1)}, f32[8,32,128]{2,1,0:T(8,128)}, u32[]{:S(2)}) %copy-start.1) | copy-done | bytes 131096
  4.5 0.0 copy-start.2
  4.5 0.9 %copy-done.2 = s32[8,32,128]{2,1,0:T(8,128)S(1)} copy-done((s32[8,32,128]{2,1,0:T(8,128)S(1)}, s32[8,32,128]{2,1,0:T(8,128)}, u32[]{:S(2)}) %copy-start.2) | copy-done | bytes 131096
  5.4 0.0 copy-start.3
  5.4 0.8 %copy-done.3 = s32[1,1,1,8,2048]{4,3,2,1,0:T(8,128)S(1)} copy-done((s32[1,1,1,8,2048]{4,3,2,1,0:T(8,128)S(1)}, s32[1,1,1,8,2048]{4,3,2,1,0:T(8,128)}, u32[]{:S(2)}) %copy-start.3) | copy-done | bytes 65560
  6.3 0.0 copy-start.4
  6.3 0.8 %copy-done.4 = f32[1,1,1,8,2048]{4,3,2,1,0:T(8,128)S(1)} copy-done((f32[1,1,1,8,2048]{4,3,2,1,0:T(8,128)S(1)}, f32[1,1,1,8,2048]{4,3,2,1,0:T(8,128)}, u32[]{:S(2)}) %copy-start.4) | copy-done | bytes 65560
  7.1 20.1 %shard_map.121 = (f32[3,8,32,128]{3,2,1,0:T(8,128)S(1)}, f32[8,32,128]{2,1,0:T(8,128)S(1)}, f32[8,32,128]{2,1,0:T(8,128)S(1)}) custom-call(f32[3,8,32,128]{3,2,1,0:T(8,128)S(1)} %copy-done, f32[8,32,128]{2,1,0:T(8,128)S(1)} %copy-done.1, s32[8,32,128]{2,1,0:T(8,128)S(1)} %copy-done.2, f32[3,128]{1,0:T(4,128)S(1)} %bitcast.11, f32[1]{0:T(128)S(6)} %copy.19.pitch_ref, ...), custom_call_target="tpu_custom_call" | custom-call | tf_op jit(solution)/shard_map/pallas_call | solution.py:466
  27.2 0.7 %copy.20 = f32[3,8,32,128]{3,2,1,0:T(8,128)} copy(f32[3,8,32,128]{3,2,1,0:T(8,128)S(1)} %get-tuple-element.6) | data formatting | bytes 786432
  27.9 0.7 %copy.21 = f32[8,32,128]{2,1,0:T(8,128)} copy(f32[8,32,128]{2,1,0:T(8,128)S(1)} %get-tuple-element.7) | data formatting | bytes 262144
  28.6 0.7 %copy.22 = f32[8,32,128]{2,1,0:T(8,128)} copy(f32[8,32,128]{2,1,0:T(8,128)S(1)} %get-tuple-element.8) | data formatting | bytes 262144
  (1 shorter events, 0.0 us)
Async XLA Ops:
  0.6 1.4 %copy-start.5 = (s32[1,1,1,2048]{3,2,1,0:T(1,128)S(1)}, s32[1,1,1,2048]{3,2,1,0:T(1,128)}, u32[]{:S(2)}) copy-start(s32[1,1,1,2048]{3,2,1,0:T(1,128)} %param.17) | copy-start | bytes 24580
  1.3 0.7 %copy-start.8 = (f32[1,1,3,128]{3,1,2,0:T(1,128)S(1)}, f32[1,1,3,128]{3,1,2,0:T(1,128)}, u32[]{:S(2)}) copy-start(f32[1,1,3,128]{3,1,2,0:T(1,128)} %param.13) | copy-start | bytes 4612
  1.3 0.7 %copy-start.6 = (s32[1,1,1,8,128]{4,3,2,1,0:T(8,128)S(1)}, s32[1,1,1,8,128]{4,3,2,1,0:T(8,128)}, u32[]{:S(2)}) copy-start(s32[1,1,1,8,128]{4,3,2,1,0:T(8,128)} %param.16) | copy-start | bytes 12292
  2.0 0.7 %copy-start.7 = (s32[1,1,1,8]{3,2,1,0:T(1,128)S(1)}, s32[1,1,1,8]{3,2,1,0:T(1,128)}, u32[]{:S(2)}) copy-start(s32[1,1,1,8]{3,2,1,0:T(1,128)} %param.15) | copy-start | bytes 100
  2.6 1.0 %copy-start = (f32[3,8,32,128]{3,2,1,0:T(8,128)S(1)}, f32[3,8,32,128]{3,2,1,0:T(8,128)}, u32[]{:S(2)}) copy-start(f32[3,8,32,128]{3,2,1,0:T(8,128)} %vel_ref.1) | copy-start | bytes 1179652
  3.6 0.9 %copy-start.1 = (f32[8,32,128]{2,1,0:T(8,128)S(1)}, f32[8,32,128]{2,1,0:T(8,128)}, u32[]{:S(2)}) copy-start(f32[8,32,128]{2,1,0:T(8,128)} %nu_ref.1) | copy-start | bytes 393220
  4.5 0.9 %copy-start.2 = (s32[8,32,128]{2,1,0:T(8,128)S(1)}, s32[8,32,128]{2,1,0:T(8,128)}, u32[]{:S(2)}) copy-start(s32[8,32,128]{2,1,0:T(8,128)} %fluid_ref.1) | copy-start | bytes 393220
  5.4 0.8 %copy-start.3 = (s32[1,1,1,8,2048]{4,3,2,1,0:T(8,128)S(1)}, s32[1,1,1,8,2048]{4,3,2,1,0:T(8,128)}, u32[]{:S(2)}) copy-start(s32[1,1,1,8,2048]{4,3,2,1,0:T(8,128)} %param.18) | copy-start | bytes 196612
  6.3 0.8 %copy-start.4 = (f32[1,1,1,8,2048]{4,3,2,1,0:T(8,128)S(1)}, f32[1,1,1,8,2048]{4,3,2,1,0:T(8,128)}, u32[]{:S(2)}) copy-start(f32[1,1,1,8,2048]{4,3,2,1,0:T(8,128)} %param.19) | copy-start | bytes 196612

commit v2 on v1

--- a/solution.py
+++ b/solution.py
@@ -27,14 +27,43 @@
 
 def lookup(row, lanes):
     table = jnp.broadcast_to(row, lanes.shape)
-    return jnp.take_along_axis(table, lanes, axis=1, mode="promise_in_bounds")
+    return lax.gather(
+        table,
+        lanes[:, :, None],
+        lax.GatherDimensionNumbers(
+            offset_dims=(),
+            collapsed_slice_dims=(1,),
+            start_index_map=(1,),
+            operand_batching_dims=(0,),
+            start_indices_batching_dims=(0,),
+        ),
+        slice_sizes=(1, 1),
+        mode=lax.GatherScatterMode.PROMISE_IN_BOUNDS,
+    )
 
 
 def step_kernel(
     sizes,
+    vel_hbm,
+    nu_hbm,
+    fluid_hbm,
+    surf_hbm,
+    pitch_hbm,
+    tiles_hbm,
+    rows_hbm,
+    cell_hbm,
+    src_hbm,
+    weight_hbm,
+    new_vel,
+    new_nu,
+    wall_out,
+    padded,
+    edge_z,
+    wall_ref,
+    fluid_ref,
     vel_ref,
     nu_ref,
-    fluid_ref,
+    fields,
     surf_ref,
     pitch_ref,
     tiles_ref,
@@ -42,16 +71,11 @@
     cell_ref,
     src_ref,
     weight_ref,
-    new_vel_ref,
-    new_nu_ref,
-    wall_ref,
     out_buf,
     in_buf,
     points,
     inverse,
     ghost,
-    padded,
-    edge_z,
     turn,
     pack_y,
     got_y,
@@ -61,6 +85,11 @@
     flat_y,
     flat_z2,
     dist,
+    tile_of,
+    vel_sem,
+    nu_sem,
+    wall_sem,
+    load,
     peer_send,
     peer_recv,
     point_send,
@@ -68,21 +97,35 @@
     halo_send,
     halo_recv,
 ):
+    pairs = (
+        (rows_hbm, rows_ref),
+        (vel_hbm, fields.at[0:3]),
+        (nu_hbm, fields.at[3]),
+        (pitch_hbm, pitch_ref),
+        (surf_hbm, surf_ref),
+        (cell_hbm, cell_ref),
+        (src_hbm, src_ref),
+        (weight_hbm, weight_ref),
+        (tiles_hbm, tiles_ref),
+        (fluid_hbm, fluid_ref),
+    )
+    loads = [pltpu.make_async_copy(x, y, load.at[i]) for i, (x, y) in enumerate(pairs)]
+    for copy in loads:
+        copy.start()
+
     nx, ny, nz = sizes
     peers = nx * nz
-    _, cx, cy, cz = vel_ref.shape
+    _, cx, cy, cz = vel_hbm.shape
     rows_y = cy // 8
-    chunks = cell_ref.shape[1] // LANES
+    chunks = cell_hbm.shape[1] // LANES
     a, b, c = (lax.axis_index(name) for name in ("gx", "gy", "gz"))
     me = a * nz + c
-    slots = tiles_ref.shape[0]
+    lane = lax.broadcasted_iota(jnp.int32, (8, LANES), 1)
+    slots = tiles_hbm.shape[1]
     per_row = cy // TY
-    lane = lax.broadcasted_iota(jnp.int32, (8, LANES), 1)
 
     def field(f, i, start, count):
-        if f < 3:
-            return vel_ref[f, i, pl.ds(start, count), :]
-        return nu_ref[i, pl.ds(start, count), :]
+        return fields[f, i, pl.ds(start, count), :]
 
     def peer_of(d):
         other = lax.rem(me + d, peers)
@@ -98,9 +141,11 @@
     for d in range(1, ny):
         pl.semaphore_signal(barrier, inc=1, device_id=column_of(d)[1], device_id_type=MESH)
 
+    for copy in loads[0:5]:
+        copy.wait()
     angle = jnp.full((1, LANES), pitch_ref[0], jnp.float32)
     cosine, sine = jnp.cos(angle), jnp.sin(angle)
-    px, py, pz = surf_ref[0:1, :], surf_ref[1:2, :], surf_ref[2:3, :]
+    px, py, pz = surf_ref[0], surf_ref[1], surf_ref[2]
     points[b] = jnp.concatenate(
         [cosine * px + sine * pz, py, cosine * pz - sine * px, jnp.zeros((5, LANES), jnp.float32)], axis=0
     )
@@ -156,6 +201,9 @@
     for copy in point_copies:
         copy.start()
     in_buf[me] = out_buf[me]
+
+    for copy in loads[5:]:
+        copy.wait()
 
     def invert(pair, total):
         cells = cell_ref[:, pl.ds(pl.multiple_of(pair * 256, 256), 256)]
@@ -321,36 +369,50 @@
         step_z = deep - jnp.broadcast_to(points[g, 2:3, :], (LANES, LANES)).T
         flat_z2[at, :] = step_z * step_z
 
+    for s in range(slots):
+        tile_of[s] = jnp.broadcast_to(tiles_ref[0:1, s : s + 1], (8, LANES))
+
     def one_slot(s, carry):
-        tile = jnp.maximum(tiles_ref[s], 0)
-        plane = lax.div(tile, per_row).astype(jnp.float32)
+        tile = jnp.maximum(tile_of[s], 0)
+        at_x = lax.div(tile, per_row).astype(jnp.float32) + (0.5 - 0.5 * cx)
         first = lax.rem(tile, per_row) * TY + b * cy
-        at_x = jnp.full((8, LANES), plane + 0.5 - 0.5 * cx, jnp.float32)
-        at_y = [
-            jnp.full((8, LANES), (first + r).astype(jnp.float32) + 0.5 - 0.5 * (ny * cy), jnp.float32)
-            for r in range(TY)
-        ]
+        at_y = first.astype(jnp.float32) + (0.5 - 0.5 * (ny * cy))
 
         def some_points(k, best):
             for u in range(4):
                 at = pl.ds(pl.multiple_of(k * 32, 32) + 8 * u, 8)
                 step_x = at_x - flat_x[at, :]
-                both = step_x * step_x + flat_z2[at, :]
-                beside_y = flat_y[at, :]
-                new = []
-                for r in range(TY):
-                    step_y = at_y[r] - beside_y
-                    new.append(jnp.minimum(best[r], step_y * step_y + both))
+                step_y = at_y - flat_y[at, :]
+                value = (step_x * step_x + step_y * step_y) + flat_z2[at, :]
+                twice = step_y + step_y
+                new = [jnp.minimum(best[0], value)]
+                for r in range(1, TY):
+                    value = value + twice
+                    new.append(jnp.minimum(best[r], value))
                 best = tuple(new)
             return best
 
         start = tuple(jnp.full((8, LANES), jnp.inf, jnp.float32) for _ in range(TY))
         best = lax.fori_loop(0, ny * LANES // 32, some_points, start)
-        least = jnp.concatenate([jnp.min(x, axis=0, keepdims=True) for x in best], axis=0)
+        least = jnp.concatenate(
+            [jnp.min(x, axis=0, keepdims=True) + float(r * r) for r, x in enumerate(best)], axis=0
+        )
         dist[s] = jnp.minimum(jnp.sqrt(least + dist_eps), dist_cap)
         return carry
 
     lax.fori_loop(0, slots, one_slot, 0)
+
+    def place(i, carry):
+        for jb in range(rows_y):
+            wall = jnp.full((8, LANES), dist_cap, jnp.float32)
+            for s in range(slots):
+                wall = jnp.where(tile_of[s] == i * per_row + jb, dist[s], wall)
+            wall_ref[i, 8 * jb : 8 * jb + 8, :] = wall
+        return carry
+
+    lax.fori_loop(0, cx, place, 0)
+    wall_copy = pltpu.make_async_copy(wall_ref, wall_out, wall_sem)
+    wall_copy.start()
 
     for axis in range(3):
         wait_halo(axis)
@@ -367,9 +429,17 @@
             turn[LANES - 2 : LANES, :] = got_z[0, at : at + 2, :]
             edge_z[f, planes * g : planes * (g + 1), :, :] = turn[...].T.reshape(planes, cy, LANES)
 
+    def plane_copies(i):
+        return (
+            pltpu.make_async_copy(vel_ref.at[:, i], new_vel.at[:, i], vel_sem.at[i]),
+            pltpu.make_async_copy(nu_ref.at[i], new_nu.at[i], nu_sem.at[i]),
+        )
+
     def advance(i, carry):
         for jb in range(rows_y):
             advance_rows(i, jb)
+        for copy in plane_copies(i):
+            copy.start()
         return carry
 
     def advance_rows(i, jb):
@@ -403,11 +473,7 @@
         chi = positive * (1.0 / viscosity)
         chi_cubed = chi * chi * chi
         diffusion = viscosity + positive * chi_cubed / (chi_cubed + visc_coef**3)
-        wall = jnp.full((8, LANES), dist_cap, jnp.float32)
-        number = i * per_row + jb
-        for s in range(slots):
-            wall = jnp.where(tiles_ref[s] == number, dist[s], wall)
-        wall_ref[i, 8 * jb : 8 * jb + 8, :] = wall
+        wall = wall_ref[i, 8 * jb : 8 * jb + 8, :]
         arg = (8.0 * diffusion) / (rate * (karman * karman) * (wall * wall))
         shield = 1.0 - jnp.tanh(arg * arg * arg)
         length = wall - shield * jnp.maximum(wall - des_coef, 0.0)
@@ -416,7 +482,7 @@
             convect = u * gradient[0][f] + v * gradient[1][f] + w * gradient[2][f]
             if f < 3:
                 change = diffusion * laplace[f] - convect
-                new_vel_ref[f, i, 8 * jb : 8 * jb + 8, :] = center[f] + scale * change
+                vel_ref[f, i, 8 * jb : 8 * jb + 8, :] = center[f] + scale * change
             else:
                 squares = (
                     gradient[0][3] * gradient[0][3]
@@ -429,7 +495,7 @@
                     + prod_coef * rate * working
                     - wall_coef * working * jnp.abs(working) / (length * length)
                 )
-                new_nu_ref[i, 8 * jb : 8 * jb + 8, :] = working + scale * change
+                nu_ref[i, 8 * jb : 8 * jb + 8, :] = working + scale * change
 
     lax.fori_loop(0, cx, advance, 0)
 
@@ -440,6 +506,25 @@
             @pl.when(exists(axis, side))
             def _():
                 halo_copy(axis, side).wait_send()
+
+    def finish(i, carry):
+        for copy in plane_copies(i):
+            copy.wait()
+        return carry
+
+    lax.fori_loop(0, cx, finish, 0)
+    wall_copy.wait()
+
+
+def hand_over(vel, nu, wall, new_vel, new_nu, wall_out, sems):
+    copies = [
+        pltpu.make_async_copy(x, y, sems.at[i])
+        for i, (x, y) in enumerate(((vel, new_vel), (nu, new_nu), (wall, wall_out)))
+    ]
+    for copy in copies:
+        copy.start()
+    for copy in copies:
+        copy.wait()
 
 
 def on_device(
@@ -460,26 +545,39 @@
     ghosts = ghost_cell.shape[-1]
     points_dev = surface.shape[-1]
     slots = near_tiles.shape[-1]
-    vmem = pl.BlockSpec(memory_space=pltpu.VMEM)
-    smem = pl.BlockSpec(memory_space=pltpu.SMEM)
-    f32 = jnp.float32
-    return pl.pallas_call(
+    hbm = pl.BlockSpec(memory_space=pltpu.HBM)
+    f32, i32 = jnp.float32, jnp.int32
+    limit = 60 * 1024 * 1024
+    results = (
+        jax.ShapeDtypeStruct(velocity.shape, f32),
+        jax.ShapeDtypeStruct(nu_tilde.shape, f32),
+        jax.ShapeDtypeStruct(nu_tilde.shape, f32),
+    )
+    work = pl.pallas_call(
         functools.partial(step_kernel, (nx, ny, nz)),
-        out_shape=(
-            jax.ShapeDtypeStruct(velocity.shape, f32),
-            jax.ShapeDtypeStruct(nu_tilde.shape, f32),
-            jax.ShapeDtypeStruct(nu_tilde.shape, f32),
-        ),
-        in_specs=[vmem, vmem, vmem, vmem, smem, smem, vmem, vmem, vmem, vmem],
-        out_specs=(vmem, vmem, vmem),
+        out_shape=results,
+        in_specs=[hbm] * 10,
+        out_specs=(hbm,) * 3,
         scratch_shapes=[
+            pltpu.VMEM((4, cx + 4, cy + 16, cz), f32),
+            pltpu.VMEM((4, cx, cy, cz), f32),
+            pltpu.VMEM((cx, cy, cz), f32),
+            pltpu.VMEM((cx, cy, cz), i32),
+            pltpu.VMEM(velocity.shape, f32),
+            pltpu.VMEM(nu_tilde.shape, f32),
+            pltpu.VMEM((4, cx, cy, cz), f32),
+            pltpu.VMEM((3, 1, points_dev), f32),
+            pltpu.SMEM((1,), f32),
+            pltpu.VMEM((1, slots), i32),
+            pltpu.VMEM((peers, LANES), i32),
+            pltpu.VMEM((1, ghosts), i32),
+            pltpu.VMEM((8, ghosts), i32),
+            pltpu.VMEM((8, ghosts), f32),
             pltpu.VMEM((peers, 4, LANES), f32),
             pltpu.VMEM((peers, 4, LANES), f32),
             pltpu.VMEM((ny, 8, points_dev), f32),
-            pltpu.VMEM((cx, cy, 2 * LANES), jnp.int32),
+            pltpu.VMEM((cx, cy, 2 * LANES), i32),
             pltpu.VMEM((4, ghosts // LANES, LANES), f32),
-            pltpu.VMEM((4, cx + 4, cy + 16, cz), f32),
-            pltpu.VMEM((4, cx, cy, cz), f32),
             pltpu.VMEM((LANES, LANES), f32),
             pltpu.VMEM((2, 8 * cx, cz), f32),
             pltpu.VMEM((2, 8 * cx, cz), f32),
@@ -489,6 +587,11 @@
             pltpu.VMEM((ny * points_dev, cz), f32),
             pltpu.VMEM((ny * points_dev, cz), f32),
             pltpu.VMEM((slots, TY, cz), f32),
+            pltpu.VMEM((slots, TY, cz), i32),
+            pltpu.SemaphoreType.DMA((cx,)),
+            pltpu.SemaphoreType.DMA((cx,)),
+            pltpu.SemaphoreType.DMA,
+            pltpu.SemaphoreType.DMA((10,)),
             pltpu.SemaphoreType.DMA((peers,)),
             pltpu.SemaphoreType.DMA((peers,)),
             pltpu.SemaphoreType.DMA((ny,)),
@@ -497,20 +600,28 @@
             pltpu.SemaphoreType.DMA((6,)),
         ],
         compiler_params=pltpu.CompilerParams(
-            collective_id=0, has_side_effects=True, vmem_limit_bytes=40 * 1024 * 1024
+            collective_id=0, has_side_effects=True, vmem_limit_bytes=limit
         ),
     )(
         velocity,
         nu_tilde,
         fluid_cells,
-        surface[0, 0],
+        jnp.transpose(surface, (0, 2, 1, 3))[0],
         pitch_angle,
-        near_tiles[0, 0, 0],
+        near_tiles[0, 0],
         send_rows[0, 0, 0],
         ghost_cell[0, 0],
         ghost_src[0, 0, 0],
         ghost_weight[0, 0, 0],
     )
+    return pl.pallas_call(
+        hand_over,
+        out_shape=results,
+        in_specs=[hbm] * 3,
+        out_specs=(hbm,) * 3,
+        scratch_shapes=[pltpu.SemaphoreType.DMA((3,))],
+        compiler_params=pltpu.CompilerParams(vmem_limit_bytes=limit),
+    )(*work)
 
 
 def solution(mesh):

time: 29.6 us -> 42.6 us (1.44)
  Pallas kernels: 20.1 us -> 41.2 us
  local copies, waits for them, and re-layouts: 7.86 us -> 0 us
    pallas_call x1 -> x2, Pallas kernels: 20.1 us -> 41.2 us  [the longest x1 21 us: on_device(): pl.pallas_call(hand_over, out_shape=results, in_specs=[hbm] * 3, out_spec...]
    unnamed x22 -> x0, local copies, waits for them, and re-layouts: 7.86 us -> none
where the time goes in v2:
time: 42.6 us; the launch traced here: 42.5 us
  Pallas kernels  41.2 us (97%)
  between operations  1.29 us (3%)
    pallas_call x1, Pallas kernels, on_device(): pl.pallas_call(hand_over, out_shape=results, in_specs=[hbm] * 3, out_spec...  21 us
    pallas_call x1, Pallas kernels, on_device(): pl.pallas_call(functools.partial(step_kernel, (nx, ny, nz)), out_shape=re...  20.2 us

profile of v2, /device:TPU:0, one launch (start us, length us, event | category | flops | bytes accessed | tf_op | source)
XLA Modules:
  0.0 42.5 jit_solution(10941642843911815704)
XLA Ops:
  1.3 20.2 %shard_map.121 = (f32[3,8,32,128]{3,2,1,0:T(8,128)}, f32[8,32,128]{2,1,0:T(8,128)}, f32[8,32,128]{2,1,0:T(8,128)}) custom-call(f32[3,8,32,128]{3,2,1,0:T(8,128)} %vel_hbm.1, f32[8,32,128]{2,1,0:T(8,128)} %nu_hbm.1, s32[8,32,128]{2,1,0:T(8,128)} %fluid_hbm.1, f32[3,1,128]{2,1,0:T(1,128)} %bitcast.10, f32[1]{0:T(128)S(6)} %copy.13.pitch_hbm, s32[1,8]{1,0:T(1,128)} %bitcast.11, ...), custom_call_target="tpu_custom_call" | custom-call | tf_op jit(solution)/shard_map/pallas_call | solution.py:556
  21.5 21.0 %shard_map.122 = (f32[3,8,32,128]{3,2,1,0:T(8,128)}, f32[8,32,128]{2,1,0:T(8,128)}, f32[8,32,128]{2,1,0:T(8,128)}) custom-call(f32[3,8,32,128]{3,2,1,0:T(8,128)} %get-tuple-element.6.vel, f32[8,32,128]{2,1,0:T(8,128)} %get-tuple-element.7.nu, f32[8,32,128]{2,1,0:T(8,128)} %get-tuple-element.8.wall), custom_call_target="tpu_custom_call" | custom-call | tf_op jit(solution)/shard_map/pallas_call | solution.py:617

commit v3 on v2

--- a/solution.py
+++ b/solution.py
@@ -77,6 +77,8 @@
     inverse,
     ghost,
     turn,
+    by_row,
+    by_lane,
     pack_y,
     got_y,
     pack_z,
@@ -98,11 +100,11 @@
     halo_recv,
 ):
     pairs = (
+        (pitch_hbm, pitch_ref),
+        (surf_hbm, surf_ref),
         (rows_hbm, rows_ref),
         (vel_hbm, fields.at[0:3]),
         (nu_hbm, fields.at[3]),
-        (pitch_hbm, pitch_ref),
-        (surf_hbm, surf_ref),
         (cell_hbm, cell_ref),
         (src_hbm, src_ref),
         (weight_hbm, weight_ref),
@@ -141,7 +143,7 @@
     for d in range(1, ny):
         pl.semaphore_signal(barrier, inc=1, device_id=column_of(d)[1], device_id_type=MESH)
 
-    for copy in loads[0:5]:
+    for copy in loads[0:2]:
         copy.wait()
     angle = jnp.full((1, LANES), pitch_ref[0], jnp.float32)
     cosine, sine = jnp.cos(angle), jnp.sin(angle)
@@ -150,6 +152,25 @@
         [cosine * px + sine * pz, py, cosine * pz - sine * px, jnp.zeros((5, LANES), jnp.float32)], axis=0
     )
 
+    turn[...] = jnp.zeros(turn.shape, jnp.float32)
+    pl.semaphore_wait(barrier, peers - 1 + ny - 1)
+
+    def point_copy(d):
+        return pltpu.make_async_remote_copy(
+            src_ref=points.at[b],
+            dst_ref=points.at[b],
+            send_sem=point_send.at[d],
+            recv_sem=point_recv.at[d],
+            device_id=column_of(d)[1],
+            device_id_type=MESH,
+        )
+
+    point_copies = [point_copy(d) for d in range(1, ny)]
+    for copy in point_copies:
+        copy.start()
+
+    for copy in loads[2:5]:
+        copy.wait()
     groups = peers // 8
     listed = [rows_ref[8 * g : 8 * g + 8, :] for g in range(groups)]
     listed_row = [lax.shift_right_arithmetic(x, 7) for x in listed]
@@ -170,8 +191,6 @@
         for r in range(8):
             for f in range(4):
                 out_buf[8 * g + r, f : f + 1, :] = picked[4 * g + f][r : r + 1, :]
-
-    pl.semaphore_wait(barrier, peers - 1 + ny - 1)
 
     def peer_copy(d):
         other, device = peer_of(d)
@@ -184,48 +203,76 @@
             device_id_type=MESH,
         )
 
-    def point_copy(d):
-        return pltpu.make_async_remote_copy(
-            src_ref=points.at[b],
-            dst_ref=points.at[b],
-            send_sem=point_send.at[d],
-            recv_sem=point_recv.at[d],
-            device_id=column_of(d)[1],
-            device_id_type=MESH,
-        )
-
     peer_copies = [peer_copy(d) for d in range(1, peers)]
     for copy in peer_copies:
         copy.start()
-    point_copies = [point_copy(d) for d in range(1, ny)]
-    for copy in point_copies:
-        copy.start()
     in_buf[me] = out_buf[me]
 
     for copy in loads[5:]:
         copy.wait()
 
-    def invert(pair, total):
-        cells = cell_ref[:, pl.ds(pl.multiple_of(pair * 256, 256), 256)]
-        at_row = lax.shift_right_arithmetic(cells, 7)
-        at_lane = cells & (LANES - 1)
-        row_id = lax.broadcasted_iota(jnp.int32, (cx * cy, 256), 0)
-        lane_id = lax.broadcasted_iota(jnp.int32, (LANES, 256), 0)
-        number = lax.broadcasted_iota(jnp.int32, (LANES, 256), 1) + pair * 256
-        chunk_id = (lax.shift_right_arithmetic(number, 7) + 1).astype(jnp.float32)
-        place = (number & (LANES - 1)).astype(jnp.float32)
-        hit_row = jnp.where(row_id == at_row, 1.0, 0.0).astype(jnp.bfloat16)
-        hit_lane = lane_id == at_lane
-        code = jnp.concatenate(
-            [jnp.where(hit_lane, chunk_id, 0.0), jnp.where(hit_lane, place, 0.0)], axis=0
-        ).astype(jnp.bfloat16)
-        return total + lax.dot_general(
-            hit_row, code, (((1,), (1,)), ((), ())), preferred_element_type=jnp.float32
+    for copy in point_copies:
+        copy.wait_recv()
+    deep = (lax.broadcasted_iota(jnp.int32, (LANES, LANES), 1).astype(jnp.float32) + 0.5) - 0.5 * cz
+    for g in range(ny):
+        at = slice(LANES * g, LANES * (g + 1))
+        flat_x[at, :] = jnp.broadcast_to(points[g, 0:1, :], (LANES, LANES)).T
+        flat_y[at, :] = jnp.broadcast_to(points[g, 1:2, :], (LANES, LANES)).T
+        step_z = deep - jnp.broadcast_to(points[g, 2:3, :], (LANES, LANES)).T
+        flat_z2[at, :] = step_z * step_z
+
+    for s in range(slots):
+        tile_of[s] = jnp.broadcast_to(tiles_ref[0:1, s : s + 1], (8, LANES))
+
+    def one_slot(s, carry):
+        tile = jnp.maximum(tile_of[s], 0)
+        at_x = lax.div(tile, per_row).astype(jnp.float32) + (0.5 - 0.5 * cx)
+        first = lax.rem(tile, per_row) * TY + b * cy
+        at_y = first.astype(jnp.float32) + (0.5 - 0.5 * (ny * cy))
+
+        def some_points(k, best):
+            for u in range(16):
+                at = pl.ds(pl.multiple_of(k * LANES, LANES) + 8 * u, 8)
+                step_x = at_x - flat_x[at, :]
+                step_y = at_y - flat_y[at, :]
+                value = (step_x * step_x + step_y * step_y) + flat_z2[at, :]
+                twice = step_y + step_y
+                new = [jnp.minimum(best[0], value)]
+                for r in range(1, TY):
+                    value = value + twice
+                    new.append(jnp.minimum(best[r], value))
+                best = tuple(new)
+            return best
+
+        start = tuple(jnp.full((8, LANES), jnp.inf, jnp.float32) for _ in range(TY))
+        best = lax.fori_loop(0, ny, some_points, start)
+        least = jnp.concatenate(
+            [jnp.min(x, axis=0, keepdims=True) + float(r * r) for r, x in enumerate(best)], axis=0
         )
-
-    inverse[...] = lax.fori_loop(
-        0, chunks // 2, invert, jnp.zeros((cx * cy, 2 * LANES), jnp.float32)
-    ).astype(jnp.int32).reshape(cx, cy, 2 * LANES)
+        dist[s] = jnp.minimum(jnp.sqrt(least + dist_eps), dist_cap)
+        return carry
+
+    ghosts = cell_ref.shape[1]
+    cells = cell_ref[...]
+    number = lax.broadcasted_iota(jnp.int32, (1, ghosts), 1)
+    chunk_id = (lax.shift_right_arithmetic(number, 7) + 1).astype(jnp.float32)
+    in_chunk = (number & (LANES - 1)).astype(jnp.float32)
+    row_id = lax.broadcasted_iota(jnp.int32, (cx * cy, ghosts), 0)
+    lane_id = lax.broadcasted_iota(jnp.int32, (LANES, ghosts), 0)
+    hit_row = jnp.where(row_id == lax.shift_right_arithmetic(cells, 7), 1.0, 0.0)
+    hit_lane = lane_id == (cells & (LANES - 1))
+    by_row[...] = hit_row.astype(jnp.bfloat16)
+    by_lane[0:LANES, :] = jnp.where(hit_lane, chunk_id, 0.0).astype(jnp.bfloat16)
+    by_lane[LANES : 2 * LANES, :] = jnp.where(hit_lane, in_chunk, 0.0).astype(jnp.bfloat16)
+    inverse[...] = (
+        lax.dot_general(
+            by_row[...], by_lane[...], (((1,), (1,)), ((), ())), preferred_element_type=jnp.float32
+        )
+        .astype(jnp.int32)
+        .reshape(cx, cy, 2 * LANES)
+    )
+
+    lax.fori_loop(0, slots // 2, one_slot, 0)
 
     for copy in peer_copies:
         copy.wait_recv()
@@ -253,7 +300,7 @@
             ghost[f, pl.ds(m, 1), :] = -jnp.sum(weight * acc[f], axis=0, keepdims=True)
         return carry
 
-    lax.fori_loop(0, chunks, interpolate, 0)
+    lax.fori_loop(0, chunks, interpolate, 0, unroll=4 if peers <= 8 else 1)
 
     def fill(i, carry):
         for jb in range(rows_y):
@@ -359,48 +406,7 @@
         def _():
             got_z[side] = jnp.zeros(got_z.shape[1:], jnp.float32)
 
-    for copy in point_copies:
-        copy.wait_recv()
-    deep = (lax.broadcasted_iota(jnp.int32, (LANES, LANES), 1).astype(jnp.float32) + 0.5) - 0.5 * cz
-    for g in range(ny):
-        at = slice(LANES * g, LANES * (g + 1))
-        flat_x[at, :] = jnp.broadcast_to(points[g, 0:1, :], (LANES, LANES)).T
-        flat_y[at, :] = jnp.broadcast_to(points[g, 1:2, :], (LANES, LANES)).T
-        step_z = deep - jnp.broadcast_to(points[g, 2:3, :], (LANES, LANES)).T
-        flat_z2[at, :] = step_z * step_z
-
-    for s in range(slots):
-        tile_of[s] = jnp.broadcast_to(tiles_ref[0:1, s : s + 1], (8, LANES))
-
-    def one_slot(s, carry):
-        tile = jnp.maximum(tile_of[s], 0)
-        at_x = lax.div(tile, per_row).astype(jnp.float32) + (0.5 - 0.5 * cx)
-        first = lax.rem(tile, per_row) * TY + b * cy
-        at_y = first.astype(jnp.float32) + (0.5 - 0.5 * (ny * cy))
-
-        def some_points(k, best):
-            for u in range(4):
-                at = pl.ds(pl.multiple_of(k * 32, 32) + 8 * u, 8)
-                step_x = at_x - flat_x[at, :]
-                step_y = at_y - flat_y[at, :]
-                value = (step_x * step_x + step_y * step_y) + flat_z2[at, :]
-                twice = step_y + step_y
-                new = [jnp.minimum(best[0], value)]
-                for r in range(1, TY):
-                    value = value + twice
-                    new.append(jnp.minimum(best[r], value))
-                best = tuple(new)
-            return best
-
-        start = tuple(jnp.full((8, LANES), jnp.inf, jnp.float32) for _ in range(TY))
-        best = lax.fori_loop(0, ny * LANES // 32, some_points, start)
-        least = jnp.concatenate(
-            [jnp.min(x, axis=0, keepdims=True) + float(r * r) for r, x in enumerate(best)], axis=0
-        )
-        dist[s] = jnp.minimum(jnp.sqrt(least + dist_eps), dist_cap)
-        return carry
-
-    lax.fori_loop(0, slots, one_slot, 0)
+    lax.fori_loop(slots // 2, slots, one_slot, 0)
 
     def place(i, carry):
         for jb in range(rows_y):
@@ -421,13 +427,12 @@
             at = 2 * (f * cx + i)
             padded[f, i + 2, 6:8, :] = got_y[0, at : at + 2, :]
             padded[f, i + 2, 8 + cy : 10 + cy, :] = got_y[1, at : at + 2, :]
-    turn[...] = jnp.zeros(turn.shape, jnp.float32)
     for f in range(4):
         for g in range(blocks):
             at = 2 * (f * blocks + g)
-            turn[0:2, :] = got_z[1, at : at + 2, :]
-            turn[LANES - 2 : LANES, :] = got_z[0, at : at + 2, :]
-            edge_z[f, planes * g : planes * (g + 1), :, :] = turn[...].T.reshape(planes, cy, LANES)
+            turn[f * blocks + g, 0:2, :] = got_z[1, at : at + 2, :]
+            turn[f * blocks + g, LANES - 2 : LANES, :] = got_z[0, at : at + 2, :]
+            edge_z[f, planes * g : planes * (g + 1), :, :] = turn[f * blocks + g].T.reshape(planes, cy, LANES)
 
     def plane_copies(i):
         return (
@@ -516,14 +521,16 @@
     wall_copy.wait()
 
 
-def hand_over(vel, nu, wall, new_vel, new_nu, wall_out, sems):
-    copies = [
-        pltpu.make_async_copy(x, y, sems.at[i])
-        for i, (x, y) in enumerate(((vel, new_vel), (nu, new_nu), (wall, wall_out)))
-    ]
-    for copy in copies:
+def hand_over(vel, nu, wall, new_vel, new_nu, wall_out, held, come, go):
+    pieces = [(vel.at[f], new_vel.at[f]) for f in range(3)] + [(nu, new_nu), (wall, wall_out)]
+    ins = [pltpu.make_async_copy(x, held.at[i], come.at[i]) for i, (x, _) in enumerate(pieces)]
+    outs = [pltpu.make_async_copy(held.at[i], y, go.at[i]) for i, (_, y) in enumerate(pieces)]
+    for copy in ins:
         copy.start()
-    for copy in copies:
+    for first, second in zip(ins, outs):
+        first.wait()
+        second.start()
+    for copy in outs:
         copy.wait()
 
 
@@ -578,7 +585,9 @@
             pltpu.VMEM((ny, 8, points_dev), f32),
             pltpu.VMEM((cx, cy, 2 * LANES), i32),
             pltpu.VMEM((4, ghosts // LANES, LANES), f32),
-            pltpu.VMEM((LANES, LANES), f32),
+            pltpu.VMEM((4 * cx * cy // LANES, LANES, LANES), f32),
+            pltpu.VMEM((cx * cy, ghosts), jnp.bfloat16),
+            pltpu.VMEM((2 * LANES, ghosts), jnp.bfloat16),
             pltpu.VMEM((2, 8 * cx, cz), f32),
             pltpu.VMEM((2, 8 * cx, cz), f32),
             pltpu.VMEM((2, 8 * cx * cy // LANES, LANES), f32),
@@ -619,7 +628,11 @@
         out_shape=results,
         in_specs=[hbm] * 3,
         out_specs=(hbm,) * 3,
-        scratch_shapes=[pltpu.SemaphoreType.DMA((3,))],
+        scratch_shapes=[
+            pltpu.VMEM((5, cx, cy, cz), f32),
+            pltpu.SemaphoreType.DMA((5,)),
+            pltpu.SemaphoreType.DMA((5,)),
+        ],
         compiler_params=pltpu.CompilerParams(vmem_limit_bytes=limit),
     )(*work)
 

time: 42.6 us -> 23.2 us (0.54)
  Pallas kernels: 41.2 us -> 21.7 us
    pallas_call x1, Pallas kernels: 21 us -> 1.91 us  [on_device(): pl.pallas_call(hand_over, out_shape=results, in_specs=[hbm] * 3, out_spec...]
where the time goes in v3:
time: 23.2 us; the launch traced here: 23 us
  Pallas kernels  21.7 us (94%)
  between operations  1.29 us (6%)
    pallas_call x1, Pallas kernels, on_device(): pl.pallas_call(functools.partial(step_kernel, (nx, ny, nz)), out_shape=re...  19.8 us
    pallas_call x1, Pallas kernels, on_device(): pl.pallas_call(hand_over, out_shape=results, in_specs=[hbm] * 3, out_spec...  1.91 us

profile of v3, /device:TPU:0, one launch (start us, length us, event | category | flops | bytes accessed | tf_op | source)
XLA Modules:
  0.0 23.0 jit_solution(16430109149608897015)
XLA Ops:
  1.3 19.8 %shard_map.121 = (f32[3,8,32,128]{3,2,1,0:T(8,128)}, f32[8,32,128]{2,1,0:T(8,128)}, f32[8,32,128]{2,1,0:T(8,128)}) custom-call(f32[3,8,32,128]{3,2,1,0:T(8,128)} %vel_hbm.1, f32[8,32,128]{2,1,0:T(8,128)} %nu_hbm.1, s32[8,32,128]{2,1,0:T(8,128)} %fluid_hbm.1, f32[3,1,128]{2,1,0:T(1,128)} %bitcast.10, f32[1]{0:T(128)S(6)} %copy.13.pitch_hbm, s32[1,8]{1,0:T(1,128)} %bitcast.11, ...), custom_call_target="tpu_custom_call" | custom-call | tf_op jit(solution)/shard_map/pallas_call | solution.py:563
  21.1 1.9 %shard_map.122 = (f32[3,8,32,128]{3,2,1,0:T(8,128)}, f32[8,32,128]{2,1,0:T(8,128)}, f32[8,32,128]{2,1,0:T(8,128)}) custom-call(f32[3,8,32,128]{3,2,1,0:T(8,128)} %get-tuple-element.6.vel, f32[8,32,128]{2,1,0:T(8,128)} %get-tuple-element.7.nu, f32[8,32,128]{2,1,0:T(8,128)} %get-tuple-element.8.wall), custom_call_target="tpu_custom_call" | custom-call | tf_op jit(solution)/shard_map/pallas_call | solution.py:626

commit v4 on v3

--- a/solution.py
+++ b/solution.py
@@ -74,8 +74,10 @@
     out_buf,
     in_buf,
     points,
-    inverse,
-    ghost,
+    is_ghost,
+    spread,
+    choose,
+    parts,
     turn,
     by_row,
     by_lane,
@@ -126,9 +128,6 @@
     slots = tiles_hbm.shape[1]
     per_row = cy // TY
 
-    def field(f, i, start, count):
-        return fields[f, i, pl.ds(start, count), :]
-
     def peer_of(d):
         other = lax.rem(me + d, peers)
         return other, (lax.div(other, nz), b, lax.rem(other, nz))
@@ -169,28 +168,41 @@
     for copy in point_copies:
         copy.start()
 
-    for copy in loads[2:5]:
+    cells_hi = cx * cy
+    loads[2].wait()
+    row_number = lax.broadcasted_iota(jnp.int32, (cells_hi, LANES), 0)
+    lane_number = lax.broadcasted_iota(jnp.int32, (LANES, 2 * LANES), 0)
+    for p in range(peers):
+        wanted = lax.shift_right_arithmetic(rows_ref[p : p + 1, :], 7)
+        hit = jnp.where(row_number == wanted, 1.0, 0.0).astype(jnp.bfloat16)
+        choose[0:cells_hi, LANES * p : LANES * (p + 1)] = hit
+        choose[cells_hi : 2 * cells_hi, LANES * p : LANES * (p + 1)] = hit
+
+    for copy in loads[3:5]:
         copy.wait()
-    groups = peers // 8
-    listed = [rows_ref[8 * g : 8 * g + 8, :] for g in range(groups)]
-    listed_row = [lax.shift_right_arithmetic(x, 7) for x in listed]
-    listed_lane = [x & (LANES - 1) for x in listed]
-
-    def pick(i, acc):
-        acc = list(acc)
-        for j in range(cy):
-            for g in range(groups):
-                here = listed_row[g] == i * cy + j
-                for f in range(4):
-                    found = lookup(field(f, i, j, 1), listed_lane[g])
-                    acc[4 * g + f] = jnp.where(here, found, acc[4 * g + f])
-        return tuple(acc)
-
-    picked = lax.fori_loop(0, cx, pick, tuple(jnp.zeros((8, LANES), jnp.float32) for _ in range(4 * groups)))
-    for g in range(groups):
-        for r in range(8):
-            for f in range(4):
-                out_buf[8 * g + r, f : f + 1, :] = picked[4 * g + f][r : r + 1, :]
+    for f in range(4):
+        across = fields[f].reshape(cells_hi, LANES).T
+        big = across.astype(jnp.bfloat16)
+        rest = (across - big.astype(jnp.float32)).astype(jnp.bfloat16)
+        parts[LANES * f : LANES * (f + 1), 0:cells_hi] = big
+        parts[LANES * f : LANES * (f + 1), cells_hi : 2 * cells_hi] = rest
+
+    def pick(k, carry):
+        at = pl.multiple_of(k * 2 * LANES, 2 * LANES)
+        found = jnp.dot(
+            parts[...], choose[:, pl.ds(at, 2 * LANES)], preferred_element_type=jnp.float32
+        )
+        both = jnp.concatenate([rows_ref[pl.ds(2 * k, 1), :], rows_ref[pl.ds(2 * k + 1, 1), :]], axis=1)
+        here = lane_number == (both & (LANES - 1))
+        for f in range(4):
+            row = jnp.sum(
+                jnp.where(here, found[LANES * f : LANES * (f + 1), :], 0.0), axis=0, keepdims=True
+            )
+            out_buf[2 * k, f : f + 1, :] = row[:, 0:LANES]
+            out_buf[2 * k + 1, f : f + 1, :] = row[:, LANES : 2 * LANES]
+        return carry
+
+    lax.fori_loop(0, peers // 2, pick, 0, unroll=peers <= 8)
 
     def peer_copy(d):
         other, device = peer_of(d)
@@ -254,23 +266,16 @@
 
     ghosts = cell_ref.shape[1]
     cells = cell_ref[...]
-    number = lax.broadcasted_iota(jnp.int32, (1, ghosts), 1)
-    chunk_id = (lax.shift_right_arithmetic(number, 7) + 1).astype(jnp.float32)
-    in_chunk = (number & (LANES - 1)).astype(jnp.float32)
-    row_id = lax.broadcasted_iota(jnp.int32, (cx * cy, ghosts), 0)
+    row_id = lax.broadcasted_iota(jnp.int32, (cells_hi, ghosts), 0)
     lane_id = lax.broadcasted_iota(jnp.int32, (LANES, ghosts), 0)
-    hit_row = jnp.where(row_id == lax.shift_right_arithmetic(cells, 7), 1.0, 0.0)
-    hit_lane = lane_id == (cells & (LANES - 1))
-    by_row[...] = hit_row.astype(jnp.bfloat16)
-    by_lane[0:LANES, :] = jnp.where(hit_lane, chunk_id, 0.0).astype(jnp.bfloat16)
-    by_lane[LANES : 2 * LANES, :] = jnp.where(hit_lane, in_chunk, 0.0).astype(jnp.bfloat16)
-    inverse[...] = (
-        lax.dot_general(
-            by_row[...], by_lane[...], (((1,), (1,)), ((), ())), preferred_element_type=jnp.float32
-        )
-        .astype(jnp.int32)
-        .reshape(cx, cy, 2 * LANES)
-    )
+    hit_row = jnp.where(row_id == lax.shift_right_arithmetic(cells, 7), 1.0, 0.0).astype(jnp.bfloat16)
+    by_row[:, 0:ghosts] = hit_row
+    by_row[:, ghosts : 2 * ghosts] = hit_row
+    by_lane[...] = jnp.where(lane_id == (cells & (LANES - 1)), 1.0, 0.0).astype(jnp.bfloat16)
+    last_dims = (((1,), (1,)), ((), ()))
+    is_ghost[...] = lax.dot_general(
+        by_row[:, 0:ghosts], by_lane[...], last_dims, preferred_element_type=jnp.float32
+    ).reshape(cx, cy, LANES)
 
     lax.fori_loop(0, slots // 2, one_slot, 0)
 
@@ -297,23 +302,21 @@
         else:
             acc = lax.fori_loop(0, peers, one_peer, acc)
         for f in range(4):
-            ghost[f, pl.ds(m, 1), :] = -jnp.sum(weight * acc[f], axis=0, keepdims=True)
+            value = -jnp.sum(weight * acc[f], axis=0, keepdims=True)
+            big = value.astype(jnp.bfloat16)
+            rest = (value - big.astype(jnp.float32)).astype(jnp.bfloat16)
+            hit = by_lane[:, at]
+            to = pl.ds(pl.multiple_of(ghosts + m * LANES, LANES), LANES)
+            spread[LANES * f : LANES * (f + 1), at] = hit * jnp.broadcast_to(big, hit.shape)
+            spread[LANES * f : LANES * (f + 1), to] = hit * jnp.broadcast_to(rest, hit.shape)
         return carry
 
     lax.fori_loop(0, chunks, interpolate, 0, unroll=4 if peers <= 8 else 1)
 
-    def fill(i, carry):
-        for jb in range(rows_y):
-            chunk_id = inverse[i, 8 * jb : 8 * jb + 8, 0:LANES]
-            place = inverse[i, 8 * jb : 8 * jb + 8, LANES : 2 * LANES]
-            value = [field(f, i, 8 * jb, 8) for f in range(4)]
-            for m in range(chunks):
-                here = chunk_id == m + 1
-                for f in range(4):
-                    value[f] = jnp.where(here, lookup(ghost[f, m : m + 1, :], place), value[f])
-            for f in range(4):
-                padded[f, i + 2, 8 + 8 * jb : 16 + 8 * jb, :] = value[f]
-        return carry
+    stored = lax.dot_general(by_row[...], spread[...], last_dims, preferred_element_type=jnp.float32)
+    for f in range(4):
+        value = stored[:, LANES * f : LANES * (f + 1)].reshape(cx, cy, LANES)
+        padded[f, 2 : cx + 2, 8 : 8 + cy, :] = jnp.where(is_ghost[...] > 0.5, value, fields[f])
 
     low_high = ((a, nx), (b, ny), (c, nz))
 
@@ -371,10 +374,7 @@
             return padded.at[:, 0:2, 8 : 8 + cy, :] if side == 0 else padded.at[:, cx + 2 : cx + 4, 8 : 8 + cy, :]
         return (got_y, got_z)[axis - 1].at[side]
 
-    lax.fori_loop(0, 2, fill, 0)
-    lax.fori_loop(cx - 2, cx, fill, 0)
     send_halo(0)
-    lax.fori_loop(2, cx - 2, fill, 0)
     for f in range(4):
         for i in range(cx):
             at = 2 * (f * cx + i)
@@ -583,11 +583,13 @@
             pltpu.VMEM((peers, 4, LANES), f32),
             pltpu.VMEM((peers, 4, LANES), f32),
             pltpu.VMEM((ny, 8, points_dev), f32),
-            pltpu.VMEM((cx, cy, 2 * LANES), i32),
-            pltpu.VMEM((4, ghosts // LANES, LANES), f32),
+            pltpu.VMEM((cx, cy, LANES), f32),
+            pltpu.VMEM((4 * LANES, 2 * ghosts), jnp.bfloat16),
+            pltpu.VMEM((2 * cx * cy, peers * LANES), jnp.bfloat16),
+            pltpu.VMEM((4 * LANES, 2 * cx * cy), jnp.bfloat16),
             pltpu.VMEM((4 * cx * cy // LANES, LANES, LANES), f32),
-            pltpu.VMEM((cx * cy, ghosts), jnp.bfloat16),
-            pltpu.VMEM((2 * LANES, ghosts), jnp.bfloat16),
+            pltpu.VMEM((cx * cy, 2 * ghosts), jnp.bfloat16),
+            pltpu.VMEM((LANES, ghosts), jnp.bfloat16),
             pltpu.VMEM((2, 8 * cx, cz), f32),
             pltpu.VMEM((2, 8 * cx, cz), f32),
             pltpu.VMEM((2, 8 * cx * cy // LANES, LANES), f32),

time: 23.2 us -> 22.5 us (0.970)
  Pallas kernels: 21.7 us -> 21.1 us
    pallas_call x1, Pallas kernels: 19.8 us -> 19.1 us  [on_device(): pl.pallas_call(functools.partial(step_kernel, (nx, ny, nz)), out_shape=re...]
where the time goes in v4:
time: 22.5 us; the launch traced here: 22.3 us
  Pallas kernels  21.1 us (94%)
  between operations  1.29 us (6%)
    pallas_call x1, Pallas kernels, on_device(): pl.pallas_call(functools.partial(step_kernel, (nx, ny, nz)), out_shape=re...  19.1 us
    pallas_call x1, Pallas kernels, on_device(): pl.pallas_call(hand_over, out_shape=results, in_specs=[hbm] * 3, out_spec...  1.91 us

profile of v4, /device:TPU:0, one launch (start us, length us, event | category | flops | bytes accessed | tf_op | source)
XLA Modules:
  0.0 22.3 jit_solution(5307349998338478133)
XLA Ops:
  1.3 19.1 %shard_map.121 = (f32[3,8,32,128]{3,2,1,0:T(8,128)}, f32[8,32,128]{2,1,0:T(8,128)}, f32[8,32,128]{2,1,0:T(8,128)}) custom-call(f32[3,8,32,128]{3,2,1,0:T(8,128)} %vel_hbm.1, f32[8,32,128]{2,1,0:T(8,128)} %nu_hbm.1, s32[8,32,128]{2,1,0:T(8,128)} %fluid_hbm.1, f32[3,1,128]{2,1,0:T(1,128)} %bitcast.10, f32[1]{0:T(128)S(6)} %copy.13.pitch_hbm, s32[1,8]{1,0:T(1,128)} %bitcast.11, ...), custom_call_target="tpu_custom_call" | custom-call | tf_op jit(solution)/shard_map/pallas_call | solution.py:563
  20.4 1.9 %shard_map.122 = (f32[3,8,32,128]{3,2,1,0:T(8,128)}, f32[8,32,128]{2,1,0:T(8,128)}, f32[8,32,128]{2,1,0:T(8,128)}) custom-call(f32[3,8,32,128]{3,2,1,0:T(8,128)} %get-tuple-element.6.vel, f32[8,32,128]{2,1,0:T(8,128)} %get-tuple-element.7.nu, f32[8,32,128]{2,1,0:T(8,128)} %get-tuple-element.8.wall), custom_call_target="tpu_custom_call" | custom-call | tf_op jit(solution)/shard_map/pallas_call | solution.py:628

commit v5 on v4

--- a/solution.py
+++ b/solution.py
@@ -42,11 +42,10 @@
     )
 
 
-def step_kernel(
+def fill_kernel(
     sizes,
     vel_hbm,
     nu_hbm,
-    fluid_hbm,
     surf_hbm,
     pitch_hbm,
     tiles_hbm,
@@ -54,15 +53,13 @@
     cell_hbm,
     src_hbm,
     weight_hbm,
-    new_vel,
-    new_nu,
+    core,
+    halo_x,
+    halo_y,
+    halo_z,
     wall_out,
-    padded,
-    edge_z,
+    filled,
     wall_ref,
-    fluid_ref,
-    vel_ref,
-    nu_ref,
     fields,
     surf_ref,
     pitch_ref,
@@ -78,20 +75,16 @@
     spread,
     choose,
     parts,
-    turn,
     by_row,
     by_lane,
     pack_y,
-    got_y,
     pack_z,
-    got_z,
     flat_x,
     flat_y,
     flat_z2,
     dist,
     tile_of,
-    vel_sem,
-    nu_sem,
+    core_sem,
     wall_sem,
     load,
     peer_send,
@@ -111,7 +104,6 @@
         (src_hbm, src_ref),
         (weight_hbm, weight_ref),
         (tiles_hbm, tiles_ref),
-        (fluid_hbm, fluid_ref),
     )
     loads = [pltpu.make_async_copy(x, y, load.at[i]) for i, (x, y) in enumerate(pairs)]
     for copy in loads:
@@ -151,7 +143,6 @@
         [cosine * px + sine * pz, py, cosine * pz - sine * px, jnp.zeros((5, LANES), jnp.float32)], axis=0
     )
 
-    turn[...] = jnp.zeros(turn.shape, jnp.float32)
     pl.semaphore_wait(barrier, peers - 1 + ny - 1)
 
     def point_copy(d):
@@ -316,7 +307,7 @@
     stored = lax.dot_general(by_row[...], spread[...], last_dims, preferred_element_type=jnp.float32)
     for f in range(4):
         value = stored[:, LANES * f : LANES * (f + 1)].reshape(cx, cy, LANES)
-        padded[f, 2 : cx + 2, 8 : 8 + cy, :] = jnp.where(is_ghost[...] > 0.5, value, fields[f])
+        filled[f] = jnp.where(is_ghost[...] > 0.5, value, fields[f])
 
     low_high = ((a, nx), (b, ny), (c, nz))
 
@@ -329,18 +320,17 @@
         place[axis] = place[axis] + (1 if side else -1)
         return tuple(place)
 
-    def halo_copy(axis, side):
+    def halo_copy(axis, side, arrives):
         if axis == 0:
-            source = padded.at[:, 2:4, 8 : 8 + cy, :] if side == 0 else padded.at[:, cx : cx + 2, 8 : 8 + cy, :]
-            target = padded.at[:, cx + 2 : cx + 4, 8 : 8 + cy, :] if side == 0 else padded.at[:, 0:2, 8 : 8 + cy, :]
+            source = filled.at[:, 0:2] if side == 0 else filled.at[:, cx - 2 : cx]
         else:
-            pack, got = ((pack_y, got_y), (pack_z, got_z))[axis - 1]
-            source, target = pack.at[side], got.at[1 - side]
+            source = (pack_y, pack_z)[axis - 1].at[side]
+        end = side if arrives else 1 - side
         return pltpu.make_async_remote_copy(
             src_ref=source,
-            dst_ref=target,
+            dst_ref=(halo_x, halo_y, halo_z)[axis].at[end],
             send_sem=halo_send.at[2 * axis + side],
-            recv_sem=halo_recv.at[2 * axis + 1 - side],
+            recv_sem=halo_recv.at[2 * axis + end],
             device_id=beside(axis, side),
             device_id_type=MESH,
         )
@@ -349,62 +339,33 @@
         for side in range(2):
             @pl.when(exists(axis, side))
             def _():
-                halo_copy(axis, side).start()
+                halo_copy(axis, side, False).start()
 
     def wait_halo(axis):
         for side in range(2):
             @pl.when(exists(axis, side))
             def _():
-                pltpu.make_async_remote_copy(
-                    src_ref=halo_source(axis, side),
-                    dst_ref=halo_target(axis, side),
-                    send_sem=halo_send.at[2 * axis + side],
-                    recv_sem=halo_recv.at[2 * axis + side],
-                    device_id=beside(axis, side),
-                    device_id_type=MESH,
-                ).wait_recv()
-
-    def halo_source(axis, side):
-        if axis == 0:
-            return padded.at[:, 2:4, 8 : 8 + cy, :] if side == 0 else padded.at[:, cx : cx + 2, 8 : 8 + cy, :]
-        return (pack_y, pack_z)[axis - 1].at[side]
-
-    def halo_target(axis, side):
-        if axis == 0:
-            return padded.at[:, 0:2, 8 : 8 + cy, :] if side == 0 else padded.at[:, cx + 2 : cx + 4, 8 : 8 + cy, :]
-        return (got_y, got_z)[axis - 1].at[side]
+                halo_copy(axis, side, True).wait_recv()
 
     send_halo(0)
+    core_copy = pltpu.make_async_copy(filled, core, core_sem)
+    core_copy.start()
     for f in range(4):
         for i in range(cx):
             at = 2 * (f * cx + i)
-            pack_y[0, at : at + 2, :] = padded[f, i + 2, 8:10, :]
-            pack_y[1, at : at + 2, :] = padded[f, i + 2, 6 + cy : 8 + cy, :]
+            pack_y[0, at : at + 2, :] = filled[f, i, 0:2, :]
+            pack_y[1, at : at + 2, :] = filled[f, i, cy - 2 : cy, :]
     send_halo(1)
     planes = LANES // cy
     blocks = cx // planes
     for f in range(4):
         for g in range(blocks):
-            block = padded[f, 2 + planes * g : 2 + planes * (g + 1), 8 : 8 + cy, :].reshape(LANES, LANES)
+            block = filled[f, planes * g : planes * (g + 1)].reshape(LANES, LANES)
             across = block.T
             at = 2 * (f * blocks + g)
             pack_z[0, at : at + 2, :] = across[0:2, :]
             pack_z[1, at : at + 2, :] = across[LANES - 2 : LANES, :]
     send_halo(2)
-
-    for side in range(2):
-        @pl.when(jnp.logical_not(exists(0, side)))
-        def _():
-            begin = 0 if side == 0 else cx + 2
-            padded[:, begin : begin + 2, 8 : 8 + cy, :] = jnp.zeros((4, 2, cy, LANES), jnp.float32)
-
-        @pl.when(jnp.logical_not(exists(1, side)))
-        def _():
-            got_y[side] = jnp.zeros(got_y.shape[1:], jnp.float32)
-
-        @pl.when(jnp.logical_not(exists(2, side)))
-        def _():
-            got_z[side] = jnp.zeros(got_z.shape[1:], jnp.float32)
 
     lax.fori_loop(slots // 2, slots, one_slot, 0)
 
@@ -422,17 +383,103 @@
 
     for axis in range(3):
         wait_halo(axis)
-    for f in range(4):
-        for i in range(cx):
-            at = 2 * (f * cx + i)
-            padded[f, i + 2, 6:8, :] = got_y[0, at : at + 2, :]
-            padded[f, i + 2, 8 + cy : 10 + cy, :] = got_y[1, at : at + 2, :]
+    for copy in peer_copies + point_copies:
+        copy.wait_send()
+    for axis in range(3):
+        for side in range(2):
+            @pl.when(exists(axis, side))
+            def _():
+                halo_copy(axis, side, False).wait_send()
+
+    core_copy.wait()
+    wall_copy.wait()
+
+
+def step_kernel(
+    sizes,
+    core,
+    halo_x,
+    halo_y,
+    halo_z,
+    wall_hbm,
+    fluid_hbm,
+    new_vel,
+    new_nu,
+    wall_out,
+    padded,
+    got_y,
+    got_z,
+    wall_ref,
+    fluid_ref,
+    turn,
+    edge_z,
+    vel_ref,
+    nu_ref,
+    load,
+    halo_load,
+    wall_sem,
+    vel_sem,
+    nu_sem,
+):
+    cx, cy, _ = wall_ref.shape
+    rows_y = cy // 8
+    planes = LANES // cy
+    blocks = cx // planes
+    lane = lax.broadcasted_iota(jnp.int32, (8, LANES), 1)
+    place = [lax.axis_index(name) for name in ("gx", "gy", "gz")]
+    margin_x = (padded.at[:, 0:2, 8 : 8 + cy, :], padded.at[:, cx + 2 : cx + 4, 8 : 8 + cy, :])
+    targets = (margin_x, (got_y.at[0], got_y.at[1]), (got_z.at[0], got_z.at[1]))
+
+    def exists(axis, side):
+        return place[axis] > 0 if side == 0 else place[axis] < sizes[axis] - 1
+
+    def halo_copy(axis, side):
+        source = (halo_x, halo_y, halo_z)[axis].at[side]
+        return pltpu.make_async_copy(source, targets[axis][side], halo_load.at[2 * axis + side])
+
+    core_copy = pltpu.make_async_copy(core, padded.at[:, 2 : cx + 2, 8 : 8 + cy, :], load.at[0])
+    wall_copy = pltpu.make_async_copy(wall_hbm, wall_ref, load.at[1])
+    fluid_copy = pltpu.make_async_copy(fluid_hbm, fluid_ref, load.at[2])
+    for axis in (2, 1, 0):
+        for side in range(2):
+            @pl.when(exists(axis, side))
+            def _():
+                halo_copy(axis, side).start()
+
+    core_copy.start()
+    wall_copy.start()
+    fluid_copy.start()
+    for axis in (2, 1, 0):
+        for side in range(2):
+            target = targets[axis][side]
+
+            @pl.when(jnp.logical_not(exists(axis, side)))
+            def _():
+                target[...] = jnp.zeros(target.shape, jnp.float32)
+
+    for axis in (2, 1, 0):
+        for side in range(2):
+            @pl.when(exists(axis, side))
+            def _():
+                halo_copy(axis, side).wait()
+
     for f in range(4):
         for g in range(blocks):
             at = 2 * (f * blocks + g)
             turn[f * blocks + g, 0:2, :] = got_z[1, at : at + 2, :]
             turn[f * blocks + g, LANES - 2 : LANES, :] = got_z[0, at : at + 2, :]
             edge_z[f, planes * g : planes * (g + 1), :, :] = turn[f * blocks + g].T.reshape(planes, cy, LANES)
+    for f in range(4):
+        for i in range(cx):
+            at = 2 * (f * cx + i)
+            padded[f, i + 2, 6:8, :] = got_y[0, at : at + 2, :]
+            padded[f, i + 2, 8 + cy : 10 + cy, :] = got_y[1, at : at + 2, :]
+
+    core_copy.wait()
+    wall_copy.wait()
+    fluid_copy.wait()
+    show_wall = pltpu.make_async_copy(wall_ref, wall_out, wall_sem)
+    show_wall.start()
 
     def plane_copies(i):
         return (
@@ -504,34 +551,13 @@
 
     lax.fori_loop(0, cx, advance, 0)
 
-    for copy in peer_copies + point_copies:
-        copy.wait_send()
-    for axis in range(3):
-        for side in range(2):
-            @pl.when(exists(axis, side))
-            def _():
-                halo_copy(axis, side).wait_send()
-
     def finish(i, carry):
         for copy in plane_copies(i):
             copy.wait()
         return carry
 
     lax.fori_loop(0, cx, finish, 0)
-    wall_copy.wait()
-
-
-def hand_over(vel, nu, wall, new_vel, new_nu, wall_out, held, come, go):
-    pieces = [(vel.at[f], new_vel.at[f]) for f in range(3)] + [(nu, new_nu), (wall, wall_out)]
-    ins = [pltpu.make_async_copy(x, held.at[i], come.at[i]) for i, (x, _) in enumerate(pieces)]
-    outs = [pltpu.make_async_copy(held.at[i], y, go.at[i]) for i, (_, y) in enumerate(pieces)]
-    for copy in ins:
-        copy.start()
-    for first, second in zip(ins, outs):
-        first.wait()
-        second.start()
-    for copy in outs:
-        copy.wait()
+    show_wall.wait()
 
 
 def on_device(
@@ -555,23 +581,21 @@
     hbm = pl.BlockSpec(memory_space=pltpu.HBM)
     f32, i32 = jnp.float32, jnp.int32
     limit = 60 * 1024 * 1024
-    results = (
-        jax.ShapeDtypeStruct(velocity.shape, f32),
-        jax.ShapeDtypeStruct(nu_tilde.shape, f32),
-        jax.ShapeDtypeStruct(nu_tilde.shape, f32),
-    )
+    edge = 8 * cx * cy // LANES
     work = pl.pallas_call(
-        functools.partial(step_kernel, (nx, ny, nz)),
-        out_shape=results,
-        in_specs=[hbm] * 10,
-        out_specs=(hbm,) * 3,
+        functools.partial(fill_kernel, (nx, ny, nz)),
+        out_shape=(
+            jax.ShapeDtypeStruct((4, cx, cy, cz), f32),
+            jax.ShapeDtypeStruct((2, 4, 2, cy, cz), f32),
+            jax.ShapeDtypeStruct((2, 8 * cx, cz), f32),
+            jax.ShapeDtypeStruct((2, edge, LANES), f32),
+            jax.ShapeDtypeStruct((cx, cy, cz), f32),
+        ),
+        in_specs=[hbm] * 9,
+        out_specs=(hbm,) * 5,
         scratch_shapes=[
-            pltpu.VMEM((4, cx + 4, cy + 16, cz), f32),
             pltpu.VMEM((4, cx, cy, cz), f32),
             pltpu.VMEM((cx, cy, cz), f32),
-            pltpu.VMEM((cx, cy, cz), i32),
-            pltpu.VMEM(velocity.shape, f32),
-            pltpu.VMEM(nu_tilde.shape, f32),
             pltpu.VMEM((4, cx, cy, cz), f32),
             pltpu.VMEM((3, 1, points_dev), f32),
             pltpu.SMEM((1,), f32),
@@ -587,22 +611,18 @@
             pltpu.VMEM((4 * LANES, 2 * ghosts), jnp.bfloat16),
             pltpu.VMEM((2 * cx * cy, peers * LANES), jnp.bfloat16),
             pltpu.VMEM((4 * LANES, 2 * cx * cy), jnp.bfloat16),
-            pltpu.VMEM((4 * cx * cy // LANES, LANES, LANES), f32),
             pltpu.VMEM((cx * cy, 2 * ghosts), jnp.bfloat16),
             pltpu.VMEM((LANES, ghosts), jnp.bfloat16),
             pltpu.VMEM((2, 8 * cx, cz), f32),
-            pltpu.VMEM((2, 8 * cx, cz), f32),
-            pltpu.VMEM((2, 8 * cx * cy // LANES, LANES), f32),
-            pltpu.VMEM((2, 8 * cx * cy // LANES, LANES), f32),
+            pltpu.VMEM((2, edge, LANES), f32),
             pltpu.VMEM((ny * points_dev, cz), f32),
             pltpu.VMEM((ny * points_dev, cz), f32),
             pltpu.VMEM((ny * points_dev, cz), f32),
             pltpu.VMEM((slots, TY, cz), f32),
             pltpu.VMEM((slots, TY, cz), i32),
-            pltpu.SemaphoreType.DMA((cx,)),
-            pltpu.SemaphoreType.DMA((cx,)),
             pltpu.SemaphoreType.DMA,
-            pltpu.SemaphoreType.DMA((10,)),
+            pltpu.SemaphoreType.DMA,
+            pltpu.SemaphoreType.DMA((9,)),
             pltpu.SemaphoreType.DMA((peers,)),
             pltpu.SemaphoreType.DMA((peers,)),
             pltpu.SemaphoreType.DMA((ny,)),
@@ -616,7 +636,6 @@
     )(
         velocity,
         nu_tilde,
-        fluid_cells,
         jnp.transpose(surface, (0, 2, 1, 3))[0],
         pitch_angle,
         near_tiles[0, 0],
@@ -626,17 +645,32 @@
         ghost_weight[0, 0, 0],
     )
     return pl.pallas_call(
-        hand_over,
-        out_shape=results,
-        in_specs=[hbm] * 3,
+        functools.partial(step_kernel, (nx, ny, nz)),
+        out_shape=(
+            jax.ShapeDtypeStruct(velocity.shape, f32),
+            jax.ShapeDtypeStruct(nu_tilde.shape, f32),
+            jax.ShapeDtypeStruct(nu_tilde.shape, f32),
+        ),
+        in_specs=[hbm] * 6,
         out_specs=(hbm,) * 3,
         scratch_shapes=[
-            pltpu.VMEM((5, cx, cy, cz), f32),
-            pltpu.SemaphoreType.DMA((5,)),
-            pltpu.SemaphoreType.DMA((5,)),
+            pltpu.VMEM((4, cx + 4, cy + 16, cz), f32),
+            pltpu.VMEM((2, 8 * cx, cz), f32),
+            pltpu.VMEM((2, edge, LANES), f32),
+            pltpu.VMEM((cx, cy, cz), f32),
+            pltpu.VMEM((cx, cy, cz), i32),
+            pltpu.VMEM((4 * cx * cy // LANES, LANES, LANES), f32),
+            pltpu.VMEM((4, cx, cy, cz), f32),
+            pltpu.VMEM(velocity.shape, f32),
+            pltpu.VMEM(nu_tilde.shape, f32),
+            pltpu.SemaphoreType.DMA((3,)),
+            pltpu.SemaphoreType.DMA((6,)),
+            pltpu.SemaphoreType.DMA,
+            pltpu.SemaphoreType.DMA((cx,)),
+            pltpu.SemaphoreType.DMA((cx,)),
         ],
         compiler_params=pltpu.CompilerParams(vmem_limit_bytes=limit),
-    )(*work)
+    )(*work, fluid_cells)
 
 
 def solution(mesh):

time: 22.5 us -> 21.9 us (0.973)
  Pallas kernels: 21.1 us -> 20.3 us
    pallas_call x2, Pallas kernels: 21.1 us -> 20.3 us  [the longest x1 17 us: on_device(): pl.pallas_call(functools.partial(fill_kernel, (nx, ny, nz)), out_shape=(j...]
where the time goes in v5:
time: 21.9 us; the launch traced here: 21.6 us
  Pallas kernels  20.3 us (93%)
  between operations  1.29 us (6%)
    pallas_call x1, Pallas kernels, on_device(): pl.pallas_call(functools.partial(fill_kernel, (nx, ny, nz)), out_shape=(j...  17 us
    pallas_call x1, Pallas kernels, on_device(): pl.pallas_call(functools.partial(step_kernel, (nx, ny, nz)), out_shape=(j...  3.36 us

profile of v5, /device:TPU:0, one launch (start us, length us, event | category | flops | bytes accessed | tf_op | source)
XLA Modules:
  0.0 21.6 jit_solution(12570156332692382131)
XLA Ops:
  1.3 17.0 %shard_map.121 = (f32[4,8,32,128]{3,2,1,0:T(8,128)}, f32[2,4,2,32,128]{4,3,2,1,0:T(8,128)}, f32[2,64,128]{2,1,0:T(8,128)}, f32[2,16,128]{2,1,0:T(8,128)}, f32[8,32,128]{2,1,0:T(8,128)}) custom-call(f32[3,8,32,128]{3,2,1,0:T(8,128)} %vel_hbm.1, f32[8,32,128]{2,1,0:T(8,128)} %nu_hbm.1, f32[3,1,128]{2,1,0:T(1,128)} %bitcast.10, f32[1]{0:T(128)S(6)} %copy.13.pitch_hbm, ...), custom_call_target="tpu_custom_call" | custom-call | tf_op jit(solution)/shard_map/pallas_call | solution.py:585
  18.3 3.4 %shard_map.122 = (f32[3,8,32,128]{3,2,1,0:T(8,128)}, f32[8,32,128]{2,1,0:T(8,128)}, f32[8,32,128]{2,1,0:T(8,128)}) custom-call(f32[4,8,32,128]{3,2,1,0:T(8,128)} %get-tuple-element.8.core, f32[2,4,2,32,128]{4,3,2,1,0:T(8,128)} %get-tuple-element.9.halo_x, f32[2,64,128]{2,1,0:T(8,128)} %get-tuple-element.10.halo_y, f32[2,16,128]{2,1,0:T(8,128)} %get-tuple-element.11.halo_z, ...), custom_call_target="tpu_custom_call" | custom-call | tf_op jit(solution)/shard_map/pallas_call | solution.py:647

commit v6 on v5

--- a/solution.py
+++ b/solution.py
@@ -268,7 +268,8 @@
         by_row[:, 0:ghosts], by_lane[...], last_dims, preferred_element_type=jnp.float32
     ).reshape(cx, cy, LANES)
 
-    lax.fori_loop(0, slots // 2, one_slot, 0)
+    early = slots * 3 // 4
+    lax.fori_loop(0, early, one_slot, 0)
 
     for copy in peer_copies:
         copy.wait_recv()
@@ -367,7 +368,7 @@
             pack_z[1, at : at + 2, :] = across[LANES - 2 : LANES, :]
     send_halo(2)
 
-    lax.fori_loop(slots // 2, slots, one_slot, 0)
+    lax.fori_loop(early, slots, one_slot, 0)
 
     def place(i, carry):
         for jb in range(rows_y):

time: 21.9 us -> 22.3 us (1.018)
  Pallas kernels: 20.3 us -> 20.8 us
    pallas_call x1, Pallas kernels: 17 us -> 17.5 us  [on_device(): pl.pallas_call(functools.partial(fill_kernel, (nx, ny, nz)), out_shape=(j...]
where the time goes in v6:
time: 22.3 us; the launch traced here: 22.1 us
  Pallas kernels  20.8 us (93%)
  between operations  1.29 us (6%)
    pallas_call x1, Pallas kernels, on_device(): pl.pallas_call(functools.partial(fill_kernel, (nx, ny, nz)), out_shape=(j...  17.5 us
    pallas_call x1, Pallas kernels, on_device(): pl.pallas_call(functools.partial(step_kernel, (nx, ny, nz)), out_shape=(j...  3.36 us

profile of v6, /device:TPU:0, one launch (start us, length us, event | category | flops | bytes accessed | tf_op | source)
XLA Modules:
  0.0 22.1 jit_solution(5165449277475280195)
XLA Ops:
  1.3 17.5 %shard_map.121 = (f32[4,8,32,128]{3,2,1,0:T(8,128)}, f32[2,4,2,32,128]{4,3,2,1,0:T(8,128)}, f32[2,64,128]{2,1,0:T(8,128)}, f32[2,16,128]{2,1,0:T(8,128)}, f32[8,32,128]{2,1,0:T(8,128)}) custom-call(f32[3,8,32,128]{3,2,1,0:T(8,128)} %vel_hbm.1, f32[8,32,128]{2,1,0:T(8,128)} %nu_hbm.1, f32[3,1,128]{2,1,0:T(1,128)} %bitcast.10, f32[1]{0:T(128)S(6)} %copy.13.pitch_hbm, ...), custom_call_target="tpu_custom_call" | custom-call | tf_op jit(solution)/shard_map/pallas_call | solution.py:586
  18.8 3.4 %shard_map.122 = (f32[3,8,32,128]{3,2,1,0:T(8,128)}, f32[8,32,128]{2,1,0:T(8,128)}, f32[8,32,128]{2,1,0:T(8,128)}) custom-call(f32[4,8,32,128]{3,2,1,0:T(8,128)} %get-tuple-element.8.core, f32[2,4,2,32,128]{4,3,2,1,0:T(8,128)} %get-tuple-element.9.halo_x, f32[2,64,128]{2,1,0:T(8,128)} %get-tuple-element.10.halo_y, f32[2,16,128]{2,1,0:T(8,128)} %get-tuple-element.11.halo_z, ...), custom_call_target="tpu_custom_call" | custom-call | tf_op jit(solution)/shard_map/pallas_call | solution.py:648

commit v7 on v6

--- a/solution.py
+++ b/solution.py
@@ -268,7 +268,7 @@
         by_row[:, 0:ghosts], by_lane[...], last_dims, preferred_element_type=jnp.float32
     ).reshape(cx, cy, LANES)
 
-    early = slots * 3 // 4
+    early = slots // 4
     lax.fori_loop(0, early, one_slot, 0)
 
     for copy in peer_copies:

time: 22.3 us -> 21.4 us (0.960)
  Pallas kernels: 20.8 us -> 19.9 us
    pallas_call x1, Pallas kernels: 17.5 us -> 16.6 us  [on_device(): pl.pallas_call(functools.partial(fill_kernel, (nx, ny, nz)), out_shape=(j...]
where the time goes in v7:
time: 21.4 us; the launch traced here: 21.2 us
  Pallas kernels  19.9 us (93%)
  between operations  1.29 us (6%)
    pallas_call x1, Pallas kernels, on_device(): pl.pallas_call(functools.partial(fill_kernel, (nx, ny, nz)), out_shape=(j...  16.6 us
    pallas_call x1, Pallas kernels, on_device(): pl.pallas_call(functools.partial(step_kernel, (nx, ny, nz)), out_shape=(j...  3.36 us

profile of v7, /device:TPU:0, one launch (start us, length us, event | category | flops | bytes accessed | tf_op | source)
XLA Modules:
  0.0 21.2 jit_solution(5879913289203642782)
XLA Ops:
  1.3 16.6 %shard_map.121 = (f32[4,8,32,128]{3,2,1,0:T(8,128)}, f32[2,4,2,32,128]{4,3,2,1,0:T(8,128)}, f32[2,64,128]{2,1,0:T(8,128)}, f32[2,16,128]{2,1,0:T(8,128)}, f32[8,32,128]{2,1,0:T(8,128)}) custom-call(f32[3,8,32,128]{3,2,1,0:T(8,128)} %vel_hbm.1, f32[8,32,128]{2,1,0:T(8,128)} %nu_hbm.1, f32[3,1,128]{2,1,0:T(1,128)} %bitcast.10, f32[1]{0:T(128)S(6)} %copy.13.pitch_hbm, ...), custom_call_target="tpu_custom_call" | custom-call | tf_op jit(solution)/shard_map/pallas_call | solution.py:586
  17.8 3.4 %shard_map.122 = (f32[3,8,32,128]{3,2,1,0:T(8,128)}, f32[8,32,128]{2,1,0:T(8,128)}, f32[8,32,128]{2,1,0:T(8,128)}) custom-call(f32[4,8,32,128]{3,2,1,0:T(8,128)} %get-tuple-element.8.core, f32[2,4,2,32,128]{4,3,2,1,0:T(8,128)} %get-tuple-element.9.halo_x, f32[2,64,128]{2,1,0:T(8,128)} %get-tuple-element.10.halo_y, f32[2,16,128]{2,1,0:T(8,128)} %get-tuple-element.11.halo_z, ...), custom_call_target="tpu_custom_call" | custom-call | tf_op jit(solution)/shard_map/pallas_call | solution.py:648
